TPU v7x, 32 devices: a whole 2x2x4 slice. The times are simulated.
32 devices in a mesh: lon: 8 (over y, x, core), lat: 4 (over z).
Axes of the slice: x: 2, y: 2, z: 4, core: 2. Of those that a mesh axis runs over, the one named last changes fastest.
Arguments:
- concentration: float32 [72, 8, 64, 1024], P(None, None, 'lat', 'lon'), may hold values from -0.3 to 0.3
- adjoint: float32 [72, 8, 64, 1024], P(None, None, 'lat', 'lon'), may hold values from -4 to 4
- wind_east: float32 [72, 64, 1024], P(None, 'lat', 'lon'), may hold values from -0.45 to 0.45
- wind_north: float32 [72, 64, 1024], P(None, 'lat', 'lon'), may hold values from -0.45 to 0.45
- mixing: float32 [72, 64, 1024], P(None, 'lat', 'lon'), may hold values from 0.01 to 100
- sound_col: int32 [1, 32, 1024], P(None, ('lon', 'lat')), may hold values from -1 to 2047, as said below
- kernel: float32 [72, 32, 1024], P(None, ('lon', 'lat')), may hold values from 0.5 to 3
- observed: float32 [1, 32, 1024], P(None, ('lon', 'lat')), may hold values from -12 to 12
- obs_error: float32 [1, 32, 1024], P(None, ('lon', 'lat')), may hold values from 1 to 3
Outputs:
- adjoint_out: float32 [72, 8, 64, 1024], P(None, None, 'lat', 'lon')
- residual: float32 [1, 32, 1024], P(None, ('lon', 'lat'))
Inputs may be any that keep to these rules, and one draw needn't show every extreme that they name: `sound_col`: each entry is a column index inside the brick of its slot (slots b * 32 to b * 32 + 31 of an owner belong to brick b in lon-major order), or -1 for an empty slot; for each owner and brick the used slots come first. In every draw some brick receives 32 soundings from every owner.
All inputs are finite; a program needn't handle non-finite values.
Results may differ from a plain program's by a relative error of at most 0.00022.
Values sent between devices are 32-bit elements; how exact they have to be, the bound alone decides.
No kernel may reach another device: no remote copies, remote signals or barrier semaphores. Data moves between devices by JAX's collectives and lax.ppermute only.
A program may use at most 192 MiB of HBM per device.

v0:
```python
import functools

import jax
import jax.numpy as jnp
from jax import lax
from jax.experimental import pallas as pl
from jax.experimental.pallas import tpu as pltpu
from jax.sharding import PartitionSpec as P

LANES = 128
SUB = 8
MIB = 1 << 20


def rim_chunks(level_count):
    chunks = -(-level_count // 63)
    return chunks, -(-level_count // chunks)


def lane_iota():
    return lax.broadcasted_iota(jnp.int32, (SUB, LANES), 1)


def sub_iota():
    return lax.broadcasted_iota(jnp.int32, (SUB, LANES), 0)


def call(body, out_shapes, scratch, vmem_mib, flops, bytes_accessed, name):
    return pl.pallas_call(
        body,
        out_shape=out_shapes,
        scratch_shapes=scratch,
        compiler_params=pltpu.CompilerParams(vmem_limit_bytes=vmem_mib * MIB),
        cost_estimate=pl.CostEstimate(
            flops=flops, bytes_accessed=bytes_accessed, transcendentals=0
        ),
        name=name,
    )


def f32(*shape):
    return jax.ShapeDtypeStruct(shape, jnp.float32)


def put_rim(value, lane, q, chunk, rows, east_ref, west_ref):
    turned = pltpu.roll(value, 2 * q + 2, 1)
    east_ref[chunk, rows, :] = jnp.where(lane == 2 * q + 1, turned, east_ref[chunk, rows, :])
    if west_ref is not None:
        west_ref[chunk, rows, :] = jnp.where(lane == 2 * q + 2, turned, west_ref[chunk, rows, :])


def put_rows(field_ref, north_ref, south_ref, row_count, count):
    def body(i, carry):
        start = pl.multiple_of(i * SUB, SUB)
        first = start * row_count
        if south_ref is not None:
            south_ref[pl.ds(start, SUB), :] = field_ref[pl.ds(first, SUB, stride=row_count), :]
        if north_ref is not None:
            north_ref[pl.ds(start, SUB), :] = field_ref[
                pl.ds(first + row_count - 1, SUB, stride=row_count), :
            ]
        return carry

    lax.fori_loop(0, count // SUB, body, 0)


def first_rims(levels, tracers, rows, chunks, per_chunk, field, east, north, e_ref, w_ref, s_ref, n_ref):
    lane = lane_iota()
    e_ref[...] = jnp.zeros(e_ref.shape, jnp.float32)
    w_ref[...] = jnp.zeros(w_ref.shape, jnp.float32)
    plane = tracers * rows
    for chunk in range(chunks):
        def body(q, carry, chunk=chunk):
            k = chunk * per_chunk + q
            for r in range(0, plane, SUB):
                at = pl.multiple_of(k * plane + r, SUB)
                put_rim(field[pl.ds(at, SUB), :], lane, q, chunk, pl.ds(r, SUB), e_ref, w_ref)
            for r in range(0, rows, SUB):
                at = pl.multiple_of(k * rows + r, SUB)
                put_rim(east[pl.ds(at, SUB), :], lane, q, chunk, pl.ds(plane + r, SUB), e_ref, None)
            return carry

        lax.fori_loop(0, min(per_chunk, levels - chunk * per_chunk), body, 0)
    put_rows(field, n_ref.at[pl.ds(0, levels * tracers)], s_ref, rows, levels * tracers)
    put_rows(north, n_ref.at[pl.ds(levels * tracers, levels)], None, rows, levels)


def coefficients(levels, rows, per_chunk, east, north, mixing, east_rim, south_rim, *outs):
    stay, from_e, from_w, from_n, from_s, below, above = outs
    lane, sub = lane_iota(), sub_iota()
    halves = rows // SUB

    def body(k, carry):
        chunk, q = k // per_chunk, k % per_chunk
        has_up = (k < levels - 1).astype(jnp.float32)
        new = []
        tops = []
        for h in range(halves):
            at = pl.multiple_of(k * rows + h * SUB, SUB)
            blk = pl.ds(at, SUB)
            down, factor = carry[h]
            up = mixing[blk, :] * has_up
            pivot = 1.0 + up + down - down * factor
            inv = 1.0 / pivot
            next_factor = up * inv
            e = east[blk, :]
            n = north[blk, :]
            rim = pltpu.roll(east_rim[chunk, pl.ds(h * SUB, SUB), :], LANES - 1 - 2 * q, 1)
            w_in = jnp.minimum(jnp.where(lane == 0, rim, pltpu.roll(e, 1, 1)), 0.0)
            if h == 0:
                edge = south_rim[pl.ds(k, 1), :]
            else:
                edge = tops[h - 1]
            tops.append(n[SUB - 1 : SUB, :])
            s_in = jnp.minimum(
                jnp.where(sub == 0, jnp.broadcast_to(edge, (SUB, LANES)), pltpu.roll(n, 1, 0)), 0.0
            )
            e_out = jnp.maximum(e, 0.0)
            n_out = jnp.maximum(n, 0.0)
            stay[blk, :] = (1.0 - e_out + w_in - n_out + s_in) * inv
            from_e[blk, :] = e_out * inv
            from_w[blk, :] = -(w_in * inv)
            from_n[blk, :] = n_out * inv
            from_s[blk, :] = -(s_in * inv)
            below[blk, :] = down * inv
            above[blk, :] = next_factor
            new.append((up, next_factor))
        return tuple(new)

    zero = jnp.zeros((SUB, LANES), jnp.float32)
    lax.fori_loop(0, levels, body, tuple((zero, zero) for _ in range(halves)))


def step(levels, tracers, rows, chunks, per_chunk, rims_out, spread, *refs):
    refs = list(refs)
    field, east_in, west_in, north_in, south_in = refs[:5]
    stay, from_e, from_w, from_n, from_s, below, above = refs[5:12]
    refs = refs[12:]
    base = refs.pop(0) if spread else None
    out = refs.pop(0)
    if rims_out:
        e_ref, w_ref, s_ref, n_ref = refs[:4]
        refs = refs[4:]
    rim = refs.pop(0)
    solved = refs.pop(0) if spread else out
    lane, sub = lane_iota(), sub_iota()
    plane = tracers * rows
    halves = rows // SUB

    for chunk in range(chunks):
        for r in range(0, plane, SUB):
            rr = pl.ds(r, SUB)
            rim[chunk, rr, :] = jnp.where(
                lane % 2 == 1, east_in[chunk, rr, :], pltpu.roll(west_in[chunk, rr, :], LANES - 2, 1)
            )

    def forward(k, carry):
        chunk, q = k // per_chunk, k % per_chunk
        turn = LANES - 1 - 2 * q
        co = []
        for h in range(halves):
            blk = pl.ds(pl.multiple_of(k * rows + h * SUB, SUB), SUB)
            co.append(tuple(c[blk, :] for c in (stay, from_e, from_w, from_n, from_s, below)))
        new = []
        for t in range(tracers):
            edge_n = north_in[pl.ds(k * tracers + t, 1), :]
            edge_s = south_in[pl.ds(k * tracers + t, 1), :]
            for h in range(halves):
                r = t * rows + h * SUB
                at = k * plane + r
                cell = field[pl.ds(pl.multiple_of(at, SUB), SUB), :]
                side = pltpu.roll(rim[chunk, pl.ds(r, SUB), :], turn, 1)
                e = jnp.where(lane == LANES - 1, side, pltpu.roll(cell, LANES - 1, 1))
                w = jnp.where(lane == 0, side, pltpu.roll(cell, 1, 1))
                if h == halves - 1:
                    n = jnp.where(
                        sub == SUB - 1, jnp.broadcast_to(edge_n, (SUB, LANES)), pltpu.roll(cell, SUB - 1, 0)
                    )
                else:
                    n = field[pl.ds(at + 1, SUB), :]
                if h == 0:
                    s = jnp.where(sub == 0, jnp.broadcast_to(edge_s, (SUB, LANES)), pltpu.roll(cell, 1, 0))
                else:
                    s = field[pl.ds(at - 1, SUB), :]
                c0, ce, cw, cn, cs, a = co[h]
                value = (c0 * cell + ce * e) + (cw * w + cn * n) + (cs * s + a * carry[t * halves + h])
                solved[pl.ds(pl.multiple_of(at, SUB), SUB), :] = value
                new.append(value)
        return tuple(new)

    zero = jnp.zeros((SUB, LANES), jnp.float32)
    lax.fori_loop(0, levels, forward, (zero,) * (tracers * halves))

    if rims_out:
        e_ref[...] = jnp.zeros(e_ref.shape, jnp.float32)
        w_ref[...] = jnp.zeros(w_ref.shape, jnp.float32)

    def backward(i, carry):
        k = levels - 1 - i
        chunk, q = k // per_chunk, k % per_chunk
        new = []
        for h in range(halves):
            f = above[pl.ds(pl.multiple_of(k * rows + h * SUB, SUB), SUB), :]
            for t in range(tracers):
                r = t * rows + h * SUB
                blk = pl.ds(pl.multiple_of(k * plane + r, SUB), SUB)
                value = solved[blk, :] + f * carry[h * tracers + t]
                if not spread:
                    out[blk, :] = value
                if rims_out:
                    put_rim(value, lane, q, chunk, pl.ds(r, SUB), e_ref, w_ref)
                new.append(value)
            if spread:
                for t in range(spread):
                    blk = pl.ds(pl.multiple_of(k * rows * spread + t * rows + h * SUB, SUB), SUB)
                    out[blk, :] = base[blk, :] + new[-1]
        return tuple(new)

    lax.fori_loop(0, levels, backward, (zero,) * (tracers * halves))
    if rims_out:
        put_rows(out, n_ref, s_ref, rows, levels * tracers)


def pack(levels, lon_count, kernel, columns, observed, errors, out):
    per_level = columns.shape[0]
    width = per_level // lon_count
    for i in range(lon_count):
        for m in range(width):
            row = i * width + m
            lanes = pl.ds(m * LANES, LANES)
            out[i, pl.ds(0, levels), lanes] = kernel[pl.ds(row, levels, stride=per_level), :]
            out[i, pl.ds(levels, SUB), lanes] = jnp.concatenate(
                [
                    columns[pl.ds(row, 1), :].astype(jnp.float32),
                    observed[pl.ds(row, 1), :],
                    errors[pl.ds(row, 1), :],
                    jnp.zeros((SUB - 3, LANES), jnp.float32),
                ],
                axis=0,
            )


def repack(rows, lon_count, lat_count, cap, arrived, out):
    lane = lane_iota()
    per_vector = LANES // cap

    def body(b, carry):
        blk = pl.ds(pl.multiple_of(b * SUB, SUB), SUB)
        for j in range(lat_count):
            for col in range(lon_count // per_vector):
                made = None
                for g in range(per_vector):
                    i = col * per_vector + g
                    at = j * cap
                    piece = arrived[i, blk, pl.ds(at // LANES * LANES, LANES)]
                    shift = (g * cap - at % LANES) % LANES
                    if shift:
                        piece = pltpu.roll(piece, shift, 1)
                    made = piece if made is None else jnp.where(lane >= g * cap, piece, made)
                out[j, blk, pl.ds(col * LANES, LANES)] = made
        return carry

    lax.fori_loop(0, rows // SUB, body, 0)


def tracer_sum(concentration, high, low):
    total = jnp.sum(concentration[...], axis=1)
    total = total.reshape(total.shape[0] * total.shape[1], total.shape[2])
    top = total.astype(jnp.bfloat16)
    high[...] = top
    low[...] = (total - top.astype(jnp.float32)).astype(jnp.bfloat16)


def soundings(
    levels, rows, lon_count, lat_count, cap, chunks, per_chunk,
    arrived, high, low, forcing, e_ref, w_ref, s_ref, n_ref, back, table, scaled
):
    width = lon_count * cap
    blocks = levels // SUB
    row_index = lax.broadcasted_iota(jnp.int32, (rows, width), 0)
    cell_index = lax.broadcasted_iota(jnp.int32, (LANES, width), 0)

    def row_mask(j):
        col = arrived[j, pl.ds(levels, 1), :].astype(jnp.int32)
        return row_index == (col >> 7)

    for j in range(lat_count):
        col = arrived[j, pl.ds(levels, 1), :].astype(jnp.int32)
        lookup = jnp.where(cell_index == (col & (LANES - 1)), 1.0, 0.0).astype(jnp.bfloat16)
        table[j, :, :] = lookup

        def gather(b, total, j=j):
            blk = pl.ds(pl.multiple_of(b * SUB * rows, SUB * rows), SUB * rows)
            look = table[j, :, :]
            seen = jnp.dot(high[blk, :], look, preferred_element_type=jnp.float32)
            seen += jnp.dot(low[blk, :], look, preferred_element_type=jnp.float32)
            weight = arrived[j, pl.ds(pl.multiple_of(b * SUB, SUB), SUB), :]
            for kk in range(SUB):
                total += weight[kk : kk + 1, :] * seen[kk * rows : (kk + 1) * rows, :]
            return total

        total = lax.fori_loop(0, blocks, gather, jnp.zeros((rows, width), jnp.float32))
        modelled = jnp.sum(jnp.where(row_mask(j), total, 0.0), axis=0, keepdims=True)
        observed = arrived[j, pl.ds(levels + 1, 1), :]
        error = arrived[j, pl.ds(levels + 2, 1), :]
        residual = jnp.where(col >= 0, (modelled - observed) / error, 0.0)
        scaled[pl.ds(j, 1), :] = residual / error
        for i in range(lon_count):
            at = i * cap
            piece = residual[:, at // LANES * LANES : at // LANES * LANES + LANES]
            if at % LANES:
                piece = pltpu.roll(piece, LANES - at % LANES, 1)
            back[pl.ds(i * lat_count + j, 1), :] = piece

    def scatter(b, carry):
        total = jnp.zeros((SUB * rows, LANES), jnp.float32)
        for j in range(lat_count):
            weight = arrived[j, pl.ds(pl.multiple_of(b * SUB, SUB), SUB), :] * scaled[pl.ds(j, 1), :]
            top = weight.astype(jnp.bfloat16).astype(jnp.float32)
            mask = row_mask(j)
            for part in (top, weight - top):
                spread = jnp.concatenate(
                    [jnp.where(mask, part[kk : kk + 1, :], 0.0) for kk in range(SUB)], axis=0
                ).astype(jnp.bfloat16)
                total += lax.dot_general(
                    spread, table[j, :, :], (((1,), (1,)), ((), ())), preferred_element_type=jnp.float32
                )
        forcing[pl.ds(pl.multiple_of(b * SUB * rows, SUB * rows), SUB * rows), :] = total
        return carry

    lax.fori_loop(0, blocks, scatter, 0)

    lane = lane_iota()
    e_ref[...] = jnp.zeros(e_ref.shape, jnp.float32)
    w_ref[...] = jnp.zeros(w_ref.shape, jnp.float32)
    for chunk in range(chunks):
        def body(q, carry, chunk=chunk):
            for r in range(0, rows, SUB):
                at = pl.multiple_of((chunk * per_chunk + q) * rows + r, SUB)
                put_rim(forcing[pl.ds(at, SUB), :], lane, q, chunk, pl.ds(r, SUB), e_ref, w_ref)
            return carry

        lax.fori_loop(0, min(per_chunk, levels - chunk * per_chunk), body, 0)
    put_rows(forcing, n_ref, s_ref, rows, levels)


def unpack(lon_count, lat_count, cap, arrived, out):
    lane = lax.broadcasted_iota(jnp.int32, (1, LANES), 1)
    per_vector = LANES // cap
    for row in range(out.shape[0]):
        made = None
        for g in range(per_vector):
            piece = arrived[pl.ds(row * per_vector + g, 1), :]
            if g:
                piece = pltpu.roll(piece, g * cap, 1)
            made = piece if made is None else jnp.where(lane >= g * cap, piece, made)
        out[pl.ds(row, 1), :] = made


def shift(value, axis, by, ring):
    count = lax.axis_size(axis)
    if ring:
        pairs = [(i, (i + by) % count) for i in range(count)]
    else:
        pairs = [(i, i + by) for i in range(count) if 0 <= i + by < count]
    return lax.ppermute(value, axis, pairs)


def exchange(east_rim, west_rim, south_rim, north_rim):
    return (
        shift(east_rim, "lon", 1, True),
        shift(west_rim, "lon", -1, True),
        shift(south_rim, "lat", -1, False),
        shift(north_rim, "lat", 1, False),
    )


def per_device(
    concentration, adjoint, wind_east, wind_north, mixing, sound_col, kernel, observed, obs_error
):
    levels, tracers, rows, cols = adjoint.shape
    lon_count, lat_count = lax.axis_size("lon"), lax.axis_size("lat")
    slots = sound_col.shape[2]
    cap = slots // (lon_count * lat_count)
    chunks, per_chunk = rim_chunks(levels)
    plane = tracers * rows
    sent_rows = levels + SUB
    per_level = slots // LANES
    field_bytes = levels * plane * cols * 4

    def flat(x):
        return x.reshape(-1, LANES)

    packed = call(
        functools.partial(pack, levels, lon_count),
        f32(lon_count, sent_rows, lat_count * cap), (), 8, 10, 800000, "pack",
    )(flat(kernel), flat(sound_col), flat(observed), flat(obs_error))
    by_lon = lax.all_to_all(packed, "lon", split_axis=0, concat_axis=0, tiled=True)

    field = flat(adjoint)
    east, north, mix = flat(wind_east), flat(wind_north), flat(mixing)
    rims = call(
        functools.partial(first_rims, levels, tracers, rows, chunks, per_chunk),
        (
            f32(chunks, plane + rows, LANES), f32(chunks, plane, LANES),
            f32(levels * tracers, LANES), f32(levels * tracers + levels, LANES),
        ),
        (), 16, field_bytes, 2 * field_bytes, "first_rims",
    )(field, east, north)
    from_west, from_east, from_north, from_south = exchange(*rims)

    by_lat = call(
        functools.partial(repack, sent_rows, lon_count, lat_count, cap),
        f32(lat_count, sent_rows, lon_count * cap), (), 8, 10, 800000, "repack",
    )(by_lon)
    arrived = lax.all_to_all(by_lat, "lat", split_axis=0, concat_axis=0, tiled=True)

    level_block = SUB
    high, low = pl.pallas_call(
        tracer_sum,
        grid=(levels // level_block,),
        in_specs=[pl.BlockSpec((level_block, tracers, rows, cols), lambda i: (i, 0, 0, 0))],
        out_specs=[pl.BlockSpec((level_block * rows, cols), lambda i: (i, 0))] * 2,
        out_shape=[jax.ShapeDtypeStruct((levels * rows, cols), jnp.bfloat16)] * 2,
        compiler_params=pltpu.CompilerParams(vmem_limit_bytes=8 * MIB),
        cost_estimate=pl.CostEstimate(
            flops=field_bytes // 4, bytes_accessed=field_bytes, transcendentals=0
        ),
        name="tracer_sum",
    )(concentration)

    weights = call(
        functools.partial(coefficients, levels, rows, per_chunk),
        (f32(levels * rows, LANES),) * 7, (), 12, field_bytes * 2, field_bytes * 2, "coefficients",
    )(
        east, north, mix,
        lax.slice_in_dim(from_west, plane, plane + rows, axis=1),
        lax.slice_in_dim(from_south, levels * tracers, levels * tracers + levels, axis=0),
    )

    def rim_shapes(count):
        return (
            f32(chunks, count * rows, LANES), f32(chunks, count * rows, LANES),
            f32(levels * count, LANES), f32(levels * count, LANES),
        )

    def advance(value, rims, count, rims_out, base=None):
        spread = tracers if base is not None else 0
        out = f32(levels * (spread or count) * rows, LANES)
        scratch = [pltpu.VMEM((chunks, count * rows, LANES), jnp.float32)]
        if spread:
            scratch.append(pltpu.VMEM((levels * rows, LANES), jnp.float32))
        return call(
            functools.partial(step, levels, count, rows, chunks, per_chunk, rims_out, spread),
            (out,) + rim_shapes(count) if rims_out else out,
            scratch, 24, field_bytes * count, field_bytes * count // 2 + 4 * field_bytes // 8 * bool(spread),
            "step",
        )(value, *rims, *weights, *(() if base is None else (base,)))

    stepped, *rims = advance(field, (from_west, from_east, from_north, from_south), tracers, True)
    finished = advance(stepped, exchange(*rims), tracers, False)

    forcing, *rest = call(
        functools.partial(soundings, levels, rows, lon_count, lat_count, cap, chunks, per_chunk),
        (f32(levels * rows, LANES),) + rim_shapes(1) + (f32(lon_count * lat_count, LANES),),
        (
            pltpu.VMEM((lat_count, LANES, lon_count * cap), jnp.bfloat16),
            pltpu.VMEM((max(lat_count, SUB), lon_count * cap), jnp.float32),
        ),
        16, field_bytes * 8, field_bytes, "soundings",
    )(arrived, high, low)
    rims, back = rest[:4], rest[4]
    stepped_forcing, *rims = advance(forcing, exchange(*rims), 1, True)

    returned = lax.all_to_all(
        back.reshape(lon_count * lat_count, 1, LANES), ("lon", "lat"),
        split_axis=0, concat_axis=0, tiled=True,
    )
    residual = call(
        functools.partial(unpack, lon_count, lat_count, cap),
        f32(per_level, LANES), (), 4, 10, 10000, "unpack",
    )(returned.reshape(lon_count * lat_count, LANES))

    result = advance(stepped_forcing, exchange(*rims), 1, False, finished)
    return result.reshape(adjoint.shape), residual.reshape(sound_col.shape)


def solution(mesh):
    field = P(None, None, "lat", "lon")
    face = P(None, "lat", "lon")
    owned = P(None, ("lon", "lat"), None)
    return jax.shard_map(
        per_device,
        mesh=mesh,
        in_specs=(field, field, face, face, face, owned, owned, owned, owned),
        out_specs=(field, owned),
        check_vma=False,
    )
```

profile of v0, /device:TPU:0, one launch (start us, length us, event | category | flops | bytes accessed | tf_op | source)
XLA Modules:
  0.0 182.3 jit_solution(1000203874458974216)
XLA Ops:
  0.6 1.0 copy-done.24
  1.6 0.7 copy-done.26
  2.3 0.7 copy-done.27
  3.0 0.7 copy-done.28
  3.7 0.8 pack.1
  4.4 5.2 %all-to-all-start = ((f32[8,80,128]{2,1,0:T(8,128)}), f32[8,80,128]{2,1,0:T(8,128)S(1)}, u32[]{:S(2)}, u32[]{:S(2)}) async-start(f32[8,80,128]{2,1,0:T(8,128)} %pack.1), calls=%async_computation | async-start | bytes 655360 | tf_op jit(solution)/shard_map/all_to_all | solution.py:398
  9.6 2.3 %copy-done.2 = f32[72,8,16,128]{3,2,1,0:T(8,128)S(1)} copy-done((f32[72,8,16,128]{3,2,1,0:T(8,128)S(1)}, f32[72,8,16,128]{3,2,1,0:T(8,128)}, u32[]{:S(2)}) %copy-start.2) | copy-done | bytes 4718616
  11.9 1.1 copy-done.11
  13.0 1.1 copy-done.13
  14.1 7.8 %first_rims.1 = (f32[2,144,128]{2,1,0:T(8,128)S(1)}, f32[2,128,128]{2,1,0:T(8,128)}, f32[576,128]{1,0:T(8,128)}, f32[648,128]{1,0:T(8,128)S(1)}) custom-call(f32[9216,128]{1,0:T(8,128)S(1)} %bitcast.14, f32[1152,128]{1,0:T(8,128)S(1)} %bitcast.16, f32[1152,128]{1,0:T(8,128)S(1)} %bitcast.18), custom_call_target="tpu_custom_call" | custom-call | flops 4718592 | bytes 9437184 | tf_op jit(solution)/shard_map/first_rims/pallas_call | solution.py:402
  21.9 3.5 %collective-permute-start.5 = (f32[648,128]{1,0:T(8,128)S(1)}, f32[648,128]{1,0:T(8,128)S(1)}, u32[]{:S(2)}, u32[]{:S(2)}) collective-permute-start(f32[648,128]{1,0:T(8,128)S(1)} %get-tuple-element.39), channel_id=1, source_target_pairs={{0,1},{1,2},{2,3},{4,5},{5,6},{6,7},{8,9},{9,10},{10,11},{12,13},{... | collective-permute-start | bytes 995336 | tf_op jit(solution)/shard_map/ppermute | solution.py:366
  25.4 1.7 repack.1
  27.1 4.1 %all-to-all-start.1 = ((f32[4,80,256]{2,1,0:T(8,128)}), f32[4,80,256]{2,1,0:T(8,128)}, u32[]{:S(2)}, u32[]{:S(2)}) async-start(f32[4,80,256]{2,1,0:T(8,128)} %repack.1), calls=%async_computation.1 | async-start | bytes 655360 | tf_op jit(solution)/shard_map/all_to_all | solution.py:416
  31.1 1.3 collective-permute-start.11
  32.4 0.3 collective-permute-start.4
  32.7 2.4 %collective-permute-start.10 = (f32[2,128,128]{2,1,0:T(8,128)}, f32[2,128,128]{2,1,0:T(8,128)S(1)}, u32[]{:S(2)}, u32[]{:S(2)}) collective-permute-start(f32[2,128,128]{2,1,0:T(8,128)} %get-tuple-element.52), channel_id=1, source_target_pairs={{0,28},{4,0},{8,4},{12,8},{16,12},{20,16},{24,20},{28,24},{1,29},{... | collective-permute-start | bytes 393224 | tf_op jit(solution)/shard_map/ppermute | solution.py:366
  35.1 2.8 %collective-permute-done.4.refs_1_ = f32[2,144,128]{2,1,0:T(8,128)S(1)} collective-permute-done((f32[2,144,128]{2,1,0:T(8,128)S(1)}, f32[2,144,128]{2,1,0:T(8,128)S(1)}, u32[]{:S(2)}, u32[]{:S(2)}) %collective-permute-start.4) | collective-permute-done | bytes 147488 | tf_op jit(solution)/shard_map/ppermute | solution.py:366
  38.0 0.7 copy-done.18
  38.7 1.1 copy-done.12
  39.8 1.1 copy-done.14
  40.8 1.1 copy-done.17
  41.9 6.0 %coefficients.1 = (f32[1152,128]{1,0:T(8,128)S(1)}, f32[1152,128]{1,0:T(8,128)S(1)}, f32[1152,128]{1,0:T(8,128)S(1)}, f32[1152,128]{1,0:T(8,128)S(1)}, f32[1152,...) custom-call(f32[1152,128]{1,0:T(8,128)S(1)} %bitcast.17, f32[1152,128]{1,0:T(8,128)S(1)} %bitcast.19, ...), custom_call_target="tpu_custom_call" | custom-call | flops 9437184 | bytes 9437184 | tf_op jit(solution)/shard_map/coefficients/pallas_call | solution.py:432
  48.0 2.5 %copy-done.3 = f32[72,8,16,128]{3,2,1,0:T(8,128)S(1)} copy-done((f32[72,8,16,128]{3,2,1,0:T(8,128)S(1)}, f32[72,8,16,128]{3,2,1,0:T(8,128)}, u32[]{:S(2)}) %copy-start.3) | copy-done | bytes 4718616
  50.5 1.0 copy-done.19
  51.5 17.4 %step.5 = (f32[9216,128]{1,0:T(8,128)S(1)}, f32[2,128,128]{2,1,0:T(8,128)}, f32[2,128,128]{2,1,0:T(8,128)}, f32[576,128]{1,0:T(8,128)}, f32[576,128]{1,0:T(8,128)}) custom-call(f32[9216,128]{1,0:T(8,128)S(1)} %bitcast.15, f32[2,144,128]{2,1,0:T(8,128)S(1)} %collective-permute-done.4.refs_1_, f32[2,128,128]{2,1,0:T(8,128)S(1)} %collective-permute-done.10.refs_2_, ...), custom_call_target="tpu_custom_call" | custom-call | flops 37748736 | bytes 18874368 | tf_op jit(solution)/shard_map/step/pallas_call | solution.py:453
  68.8 2.2 %copy-done.8 = f32[9216,128]{1,0:T(8,128)} copy-done((f32[9216,128]{1,0:T(8,128)}, f32[9216,128]{1,0:T(8,128)S(1)}, u32[]{:S(2)}) %copy-start.8) | copy-done | bytes 4718616
  71.0 1.3 collective-permute-start.14
  72.3 5.9 %collective-permute-start.15 = (f32[576,128]{1,0:T(8,128)}, f32[576,128]{1,0:T(8,128)}, u32[]{:S(2)}, u32[]{:S(2)}) collective-permute-start(f32[576,128]{1,0:T(8,128)} %get-tuple-element.58), channel_id=1, source_target_pairs={{0,1},{1,2},{2,3},{4,5},{5,6},{6,7},{8,9},{9,10},{10,11},{12,13},{... | collective-permute-start | bytes 884744 | tf_op jit(solution)/shard_map/ppermute | solution.py:366
  78.2 2.3 %copy-done.10 = f32[72,8,16,128]{3,2,1,0:T(8,128)S(1)} copy-done((f32[72,8,16,128]{3,2,1,0:T(8,128)S(1)}, f32[72,8,16,128]{3,2,1,0:T(8,128)}, u32[]{:S(2)}) %copy-start.10) | copy-done | bytes 4718616
  80.6 0.4 tracer_sum.1
  81.0 0.7 copy-done.20
  81.7 0.7 copy-done.22
  82.4 2.6 %collective-permute-start.13 = (f32[2,128,128]{2,1,0:T(8,128)}, f32[2,128,128]{2,1,0:T(8,128)}, u32[]{:S(2)}, u32[]{:S(2)}) collective-permute-start(f32[2,128,128]{2,1,0:T(8,128)} %get-tuple-element.56), channel_id=1, source_target_pairs={{0,28},{4,0},{8,4},{12,8},{16,12},{20,16},{24,20},{28,24},{1,29},{... | collective-permute-start | bytes 393224 | tf_op jit(solution)/shard_map/ppermute | solution.py:366
  85.0 1.0 copy-done.21
  86.0 1.0 copy-done.23
  86.9 16.1 %soundings.1 = (f32[1152,128]{1,0:T(8,128)S(1)}, f32[2,16,128]{2,1,0:T(8,128)S(1)}, f32[2,16,128]{2,1,0:T(8,128)S(1)}, f32[72,128]{1,0:T(8,128)S(1)}, f32[72,128]{1,0:T(8,128)S(1)}, /*index=5*/f32[32,128]{1,0:T(8,128)S(1)}) custom-call(f32[4,80,256]{2,1,0:T(8,128)} %all-to-all-done.1.arrived, bf16[1152,128]{1,0:T(8,128)(2,1)S(1)} %copy-done.21, ...), custom_call_target="tpu_custom_call" | custom-call | flops 37748736 | bytes 4718592 | tf_op jit(solution)/shard_map/soundings/pallas_call | solution.py:463
  103.0 0.6 copy-done.25
  103.6 4.1 %collective-permute-done.refs_1_ = f32[2,16,128]{2,1,0:T(8,128)S(1)} collective-permute-done((f32[2,16,128]{2,1,0:T(8,128)S(1)}, f32[2,16,128]{2,1,0:T(8,128)S(1)}, u32[]{:S(2)}, u32[]{:S(2)}) %collective-permute-start) | collective-permute-done | bytes 16416 | tf_op jit(solution)/shard_map/ppermute | solution.py:366
  107.7 1.4 collective-permute-done.1.refs_2_
  109.1 1.3 collective-permute-start.2
  110.4 4.6 %collective-permute-done.2.refs_3_ = f32[72,128]{1,0:T(8,128)S(1)} collective-permute-done((f32[72,128]{1,0:T(8,128)S(1)}, f32[72,128]{1,0:T(8,128)S(1)}, u32[]{:S(2)}, u32[]{:S(2)}) %collective-permute-start.2) | collective-permute-done | bytes 36896 | tf_op jit(solution)/shard_map/ppermute | solution.py:366
  115.0 3.9 %collective-permute-start.3 = (f32[72,128]{1,0:T(8,128)S(1)}, f32[72,128]{1,0:T(8,128)S(1)}, u32[]{:S(2)}, u32[]{:S(2)}) collective-permute-start(f32[72,128]{1,0:T(8,128)S(1)} %get-tuple-element.37), channel_id=1, source_target_pairs={{0,1},{1,2},{2,3},{4,5},{5,6},{6,7},{8,9},{9,10},{10,11},{12,13},{... | collective-permute-start | bytes 110600 | tf_op jit(solution)/shard_map/ppermute | solution.py:366
  118.9 1.6 collective-permute-done.3.refs_4_
  120.5 1.1 copy-done.5
  121.5 11.9 %step.4 = (f32[1152,128]{1,0:T(8,128)S(1)}, f32[2,16,128]{2,1,0:T(8,128)S(1)}, f32[2,16,128]{2,1,0:T(8,128)S(1)}, f32[72,128]{1,0:T(8,128)}, f32[72,128]{1,0:T(8,128)}) custom-call(f32[1152,128]{1,0:T(8,128)S(1)} %get-tuple-element.33.refs_0_, f32[2,16,128]{2,1,0:T(8,128)S(1)} %collective-permute-done.refs_1_, ...), custom_call_target="tpu_custom_call" | custom-call | flops 4718592 | bytes 2359296 | tf_op jit(solution)/shard_map/step/pallas_call | solution.py:453
  133.5 0.8 copy-done.15
  134.3 0.6 copy-done.29
  134.9 0.6 copy-done.30
  135.5 1.3 collective-permute-start.8
  136.8 5.5 %collective-permute-start.9 = (f32[72,128]{1,0:T(8,128)}, f32[72,128]{1,0:T(8,128)}, u32[]{:S(2)}, u32[]{:S(2)}) collective-permute-start(f32[72,128]{1,0:T(8,128)} %get-tuple-element.51), channel_id=1, source_target_pairs={{0,1},{1,2},{2,3},{4,5},{5,6},{6,7},{8,9},{9,10},{10,11},{12,13},{... | collective-permute-start | bytes 110600 | tf_op jit(solution)/shard_map/ppermute | solution.py:366
  142.2 5.8 %all-to-all-start.2 = ((f32[32,1,128]{2,1,0:T(1,128)}), f32[32,1,128]{2,1,0:T(1,128)S(1)}, u32[]{:S(2)}, u32[]{:S(2)}) async-start(f32[32,1,128]{2,1,0:T(1,128)} %bitcast.23), calls=%async_computation.2 | async-start | bytes 32768 | tf_op jit(solution)/shard_map/all_to_all | solution.py:475
  148.1 0.3 collective-permute-start.6
  148.4 2.4 %collective-permute-start.7 = (f32[2,16,128]{2,1,0:T(8,128)}, f32[2,16,128]{2,1,0:T(8,128)}, u32[]{:S(2)}, u32[]{:S(2)}) collective-permute-start(f32[2,16,128]{2,1,0:T(8,128)} %copy-done.29), channel_id=1, source_target_pairs={{0,28},{4,0},{8,4},{12,8},{16,12},{20,16},{24,20},{28,24},{1,29},{... | collective-permute-start | bytes 49160 | tf_op jit(solution)/shard_map/ppermute | solution.py:366
  150.8 1.1 copy-done.6
  151.9 2.3 %copy-done.9 = f32[9216,128]{1,0:T(8,128)S(1)} copy-done((f32[9216,128]{1,0:T(8,128)S(1)}, f32[9216,128]{1,0:T(8,128)}, u32[]{:S(2)}) %copy-start.9) | copy-done | bytes 4718616
  154.2 11.0 %step.6.refs_12_ = f32[9216,128]{1,0:T(8,128)S(1)} custom-call(f32[9216,128]{1,0:T(8,128)S(1)} %copy-done.9, f32[2,128,128]{2,1,0:T(8,128)} %collective-permute-done.12.refs_1_, f32[2,128,128]{2,1,0:T(8,128)} %collective-permute-done.13.refs_2_, f32[576,128]{1,0:T(8,128)} %collective-permute-done.14.refs_3_, f32[576,128]{1,0:T(8,128)} %collective-permute-done.15.refs_4_, ...), custom_call_target="tpu_custom_call" | custom-call | flops 37748736 | bytes 18874368 | tf_op jit(solution)/shard_map/step/pallas_call | solution.py:453
  165.2 0.0 copy-start
  165.2 2.2 %copy-done = f32[9216,128]{1,0:T(8,128)} copy-done((f32[9216,128]{1,0:T(8,128)}, f32[9216,128]{1,0:T(8,128)S(1)}, u32[]{:S(2)}) %copy-start) | copy-done | bytes 4718616
  167.4 0.7 unpack.1
  168.1 0.0 copy-start.1
  168.1 2.3 %copy-done.1 = f32[9216,128]{1,0:T(8,128)S(1)} copy-done((f32[9216,128]{1,0:T(8,128)S(1)}, f32[9216,128]{1,0:T(8,128)}, u32[]{:S(2)}) %copy-start.1) | copy-done | bytes 4718616
  170.5 1.1 copy-done.7
  171.5 1.1 copy-done.16
  172.6 9.7 %step.7 = f32[9216,128]{1,0:T(8,128)} custom-call(f32[1152,128]{1,0:T(8,128)S(1)} %copy-done.16, f32[2,16,128]{2,1,0:T(8,128)} %collective-permute-done.6.refs_1_, f32[2,16,128]{2,1,0:T(8,128)} %collective-permute-done.7.refs_2_, f32[72,128]{1,0:T(8,128)} %collective-permute-done.8.refs_3_, f32[72,128]{1,0:T(8,128)} %collective-permute-done.9.refs_4_, ...), custom_call_target="tpu_custom_call" | custom-call | flops 4718592 | bytes 4718592 | tf_op jit(solution)/shard_map/step/pallas_call | solution.py:453
  (49 shorter events, 0.1 us)
Async XLA Ops:
  0.6 1.0 copy-start.24
  1.6 0.7 copy-start.26
  2.3 0.7 copy-start.27
  3.0 0.7 copy-start.28
  4.4 20.9 %all-to-all-start = ((f32[8,80,128]{2,1,0:T(8,128)}), f32[8,80,128]{2,1,0:T(8,128)S(1)}, u32[]{:S(2)}, u32[]{:S(2)}) async-start(f32[8,80,128]{2,1,0:T(8,128)} %pack.1), calls=%async_computation | async-start | bytes 655360 | tf_op jit(solution)/shard_map/all_to_all | solution.py:398
  9.6 2.3 %copy-start.2 = (f32[72,8,16,128]{3,2,1,0:T(8,128)S(1)}, f32[72,8,16,128]{3,2,1,0:T(8,128)}, u32[]{:S(2)}) copy-start(f32[72,8,16,128]{3,2,1,0:T(8,128)} %param.10) | copy-start | bytes 14155780
  11.9 1.1 copy-start.11
  13.0 1.1 copy-start.13
  21.9 16.1 %collective-permute-start.5 = (f32[648,128]{1,0:T(8,128)S(1)}, f32[648,128]{1,0:T(8,128)S(1)}, u32[]{:S(2)}, u32[]{:S(2)}) collective-permute-start(f32[648,128]{1,0:T(8,128)S(1)} %get-tuple-element.39), channel_id=1, source_target_pairs={{0,1},{1,2},{2,3},{4,5},{5,6},{6,7},{8,9},{9,10},{10,11},{12,13},{... | collective-permute-start | bytes 995336 | tf_op jit(solution)/shard_map/ppermute | solution.py:366
  27.1 58.0 %all-to-all-start.1 = ((f32[4,80,256]{2,1,0:T(8,128)}), f32[4,80,256]{2,1,0:T(8,128)}, u32[]{:S(2)}, u32[]{:S(2)}) async-start(f32[4,80,256]{2,1,0:T(8,128)} %repack.1), calls=%async_computation.1 | async-start | bytes 655360 | tf_op jit(solution)/shard_map/all_to_all | solution.py:416
  31.1 16.8 %collective-permute-start.11 = (f32[576,128]{1,0:T(8,128)}, f32[576,128]{1,0:T(8,128)S(1)}, u32[]{:S(2)}, u32[]{:S(2)}) collective-permute-start(f32[576,128]{1,0:T(8,128)} %get-tuple-element.53), channel_id=1, source_target_pairs={{1,0},{2,1},{3,2},{5,4},{6,5},{7,6},{9,8},{10,9},{11,10},{13,12},{... | collective-permute-start | bytes 884744 | tf_op jit(solution)/shard_map/ppermute | solution.py:366
  32.4 5.5 %collective-permute-start.4 = (f32[2,144,128]{2,1,0:T(8,128)S(1)}, f32[2,144,128]{2,1,0:T(8,128)S(1)}, u32[]{:S(2)}, u32[]{:S(2)}) collective-permute-start(f32[2,144,128]{2,1,0:T(8,128)S(1)} %get-tuple-element.38), channel_id=1, source_target_pairs={{0,4},{4,8},{8,12},{12,16},{16,20},{20,24},{24,28},{28,0},{1,5},{5... | collective-permute-start | bytes 442376 | tf_op jit(solution)/shard_map/ppermute | solution.py:366
  32.7 15.2 %collective-permute-start.10 = (f32[2,128,128]{2,1,0:T(8,128)}, f32[2,128,128]{2,1,0:T(8,128)S(1)}, u32[]{:S(2)}, u32[]{:S(2)}) collective-permute-start(f32[2,128,128]{2,1,0:T(8,128)} %get-tuple-element.52), channel_id=1, source_target_pairs={{0,28},{4,0},{8,4},{12,8},{16,12},{20,16},{24,20},{28,24},{1,29},{... | collective-permute-start | bytes 393224 | tf_op jit(solution)/shard_map/ppermute | solution.py:366
  38.0 0.7 copy-start.18
  38.7 1.1 copy-start.12
  39.8 1.1 copy-start.14
  40.8 1.1 copy-start.17
  47.9 20.9 %copy-start.4 = (f32[1152,128]{1,0:T(8,128)}, f32[1152,128]{1,0:T(8,128)S(1)}, u32[]{:S(2)}) copy-start(f32[1152,128]{1,0:T(8,128)S(1)} %get-tuple-element.46.refs_11_) | copy-start | bytes 1769476
  47.9 2.6 %copy-start.3 = (f32[72,8,16,128]{3,2,1,0:T(8,128)S(1)}, f32[72,8,16,128]{3,2,1,0:T(8,128)}, u32[]{:S(2)}) copy-start(f32[72,8,16,128]{3,2,1,0:T(8,128)} %param.10) | copy-start | bytes 14155780
  50.5 1.0 copy-start.19
  68.8 2.2 %copy-start.8 = (f32[9216,128]{1,0:T(8,128)}, f32[9216,128]{1,0:T(8,128)S(1)}, u32[]{:S(2)}) copy-start(f32[9216,128]{1,0:T(8,128)S(1)} %get-tuple-element.54.refs_0_) | copy-start | bytes 14155780
  71.0 77.4 %collective-permute-start.14 = (f32[576,128]{1,0:T(8,128)}, f32[576,128]{1,0:T(8,128)}, u32[]{:S(2)}, u32[]{:S(2)}) collective-permute-start(f32[576,128]{1,0:T(8,128)} %get-tuple-element.57), channel_id=1, source_target_pairs={{1,0},{2,1},{3,2},{5,4},{6,5},{7,6},{9,8},{10,9},{11,10},{13,12},{... | collective-permute-start | bytes 884744 | tf_op jit(solution)/shard_map/ppermute | solution.py:366
  72.3 78.5 %collective-permute-start.15 = (f32[576,128]{1,0:T(8,128)}, f32[576,128]{1,0:T(8,128)}, u32[]{:S(2)}, u32[]{:S(2)}) collective-permute-start(f32[576,128]{1,0:T(8,128)} %get-tuple-element.58), channel_id=1, source_target_pairs={{0,1},{1,2},{2,3},{4,5},{5,6},{6,7},{8,9},{9,10},{10,11},{12,13},{... | collective-permute-start | bytes 884744 | tf_op jit(solution)/shard_map/ppermute | solution.py:366
  78.2 58.5 %collective-permute-start.12 = (f32[2,128,128]{2,1,0:T(8,128)}, f32[2,128,128]{2,1,0:T(8,128)}, u32[]{:S(2)}, u32[]{:S(2)}) collective-permute-start(f32[2,128,128]{2,1,0:T(8,128)} %get-tuple-element.55), channel_id=1, source_target_pairs={{0,4},{4,8},{8,12},{12,16},{16,20},{20,24},{24,28},{28,0},{1,5},{5... | collective-permute-start | bytes 393224 | tf_op jit(solution)/shard_map/ppermute | solution.py:366
  78.2 2.3 %copy-start.10 = (f32[72,8,16,128]{3,2,1,0:T(8,128)S(1)}, f32[72,8,16,128]{3,2,1,0:T(8,128)}, u32[]{:S(2)}) copy-start(f32[72,8,16,128]{3,2,1,0:T(8,128)} %concentration.1) | copy-start | bytes 14155780
  80.9 0.7 copy-start.20
  81.7 0.7 copy-start.22
  82.4 65.7 %collective-permute-start.13 = (f32[2,128,128]{2,1,0:T(8,128)}, f32[2,128,128]{2,1,0:T(8,128)}, u32[]{:S(2)}, u32[]{:S(2)}) collective-permute-start(f32[2,128,128]{2,1,0:T(8,128)} %get-tuple-element.56), channel_id=1, source_target_pairs={{0,28},{4,0},{8,4},{12,8},{16,12},{20,16},{24,20},{28,24},{1,29},{... | collective-permute-start | bytes 393224 | tf_op jit(solution)/shard_map/ppermute | solution.py:366
  85.0 1.0 copy-start.21
  86.0 1.0 copy-start.23
  103.0 0.6 copy-start.25
  103.6 4.1 %collective-permute-start = (f32[2,16,128]{2,1,0:T(8,128)S(1)}, f32[2,16,128]{2,1,0:T(8,128)S(1)}, u32[]{:S(2)}, u32[]{:S(2)}) collective-permute-start(f32[2,16,128]{2,1,0:T(8,128)S(1)} %get-tuple-element.34), channel_id=1, source_target_pairs={{0,4},{4,8},{8,12},{12,16},{16,20},{20,24},{24,28},{28,0},{1,5},{5... | collective-permute-start | bytes 49160 | tf_op jit(solution)/shard_map/ppermute | solution.py:366
  107.7 1.4 collective-permute-start.1
  109.1 5.8 %collective-permute-start.2 = (f32[72,128]{1,0:T(8,128)S(1)}, f32[72,128]{1,0:T(8,128)S(1)}, u32[]{:S(2)}, u32[]{:S(2)}) collective-permute-start(f32[72,128]{1,0:T(8,128)S(1)} %get-tuple-element.36), channel_id=1, source_target_pairs={{1,0},{2,1},{3,2},{5,4},{6,5},{7,6},{9,8},{10,9},{11,10},{13,12},{... | collective-permute-start | bytes 110600 | tf_op jit(solution)/shard_map/ppermute | solution.py:366
  115.0 5.5 %collective-permute-start.3 = (f32[72,128]{1,0:T(8,128)S(1)}, f32[72,128]{1,0:T(8,128)S(1)}, u32[]{:S(2)}, u32[]{:S(2)}) collective-permute-start(f32[72,128]{1,0:T(8,128)S(1)} %get-tuple-element.37), channel_id=1, source_target_pairs={{0,1},{1,2},{2,3},{4,5},{5,6},{6,7},{8,9},{9,10},{10,11},{12,13},{... | collective-permute-start | bytes 110600 | tf_op jit(solution)/shard_map/ppermute | solution.py:366
  120.5 1.1 copy-start.5
  133.5 0.8 copy-start.15
  134.3 0.6 copy-start.29
  134.9 0.6 copy-start.30
  135.5 32.6 %collective-permute-start.8 = (f32[72,128]{1,0:T(8,128)}, f32[72,128]{1,0:T(8,128)}, u32[]{:S(2)}, u32[]{:S(2)}) collective-permute-start(f32[72,128]{1,0:T(8,128)} %get-tuple-element.50), channel_id=1, source_target_pairs={{1,0},{2,1},{3,2},{5,4},{6,5},{7,6},{9,8},{10,9},{11,10},{13,12},{... | collective-permute-start | bytes 110600 | tf_op jit(solution)/shard_map/ppermute | solution.py:366
  136.8 31.3 %collective-permute-start.9 = (f32[72,128]{1,0:T(8,128)}, f32[72,128]{1,0:T(8,128)}, u32[]{:S(2)}, u32[]{:S(2)}) collective-permute-start(f32[72,128]{1,0:T(8,128)} %get-tuple-element.51), channel_id=1, source_target_pairs={{0,1},{1,2},{2,3},{4,5},{5,6},{6,7},{8,9},{9,10},{10,11},{12,13},{... | collective-permute-start | bytes 110600 | tf_op jit(solution)/shard_map/ppermute | solution.py:366
  142.2 25.2 %all-to-all-start.2 = ((f32[32,1,128]{2,1,0:T(1,128)}), f32[32,1,128]{2,1,0:T(1,128)S(1)}, u32[]{:S(2)}, u32[]{:S(2)}) async-start(f32[32,1,128]{2,1,0:T(1,128)} %bitcast.23), calls=%async_computation.2 | async-start | bytes 32768 | tf_op jit(solution)/shard_map/all_to_all | solution.py:475
  148.1 20.0 %collective-permute-start.6 = (f32[2,16,128]{2,1,0:T(8,128)}, f32[2,16,128]{2,1,0:T(8,128)}, u32[]{:S(2)}, u32[]{:S(2)}) collective-permute-start(f32[2,16,128]{2,1,0:T(8,128)} %copy-done.30), channel_id=1, source_target_pairs={{0,4},{4,8},{8,12},{12,16},{16,20},{20,24},{24,28},{28,0},{1,5},{5... | collective-permute-start | bytes 49160 | tf_op jit(solution)/shard_map/ppermute | solution.py:366
  148.4 19.7 %collective-permute-start.7 = (f32[2,16,128]{2,1,0:T(8,128)}, f32[2,16,128]{2,1,0:T(8,128)}, u32[]{:S(2)}, u32[]{:S(2)}) collective-permute-start(f32[2,16,128]{2,1,0:T(8,128)} %copy-done.29), channel_id=1, source_target_pairs={{0,28},{4,0},{8,4},{12,8},{16,12},{20,16},{24,20},{28,24},{1,29},{... | collective-permute-start | bytes 49160 | tf_op jit(solution)/shard_map/ppermute | solution.py:366
  150.8 1.1 copy-start.6
  151.9 2.3 %copy-start.9 = (f32[9216,128]{1,0:T(8,128)S(1)}, f32[9216,128]{1,0:T(8,128)}, u32[]{:S(2)}) copy-start(f32[9216,128]{1,0:T(8,128)} %copy-done.8) | copy-start | bytes 14155780
  165.2 2.2 %copy-start = (f32[9216,128]{1,0:T(8,128)}, f32[9216,128]{1,0:T(8,128)S(1)}, u32[]{:S(2)}) copy-start(f32[9216,128]{1,0:T(8,128)S(1)} %step.6.refs_12_) | copy-start | bytes 14155780
  168.1 2.3 %copy-start.1 = (f32[9216,128]{1,0:T(8,128)S(1)}, f32[9216,128]{1,0:T(8,128)}, u32[]{:S(2)}) copy-start(f32[9216,128]{1,0:T(8,128)} %copy-done) | copy-start | bytes 14155780
  170.5 1.1 copy-start.7
  171.5 1.1 copy-start.16
where the time goes:
time: 184 us; the launch traced here: 182 us
  Pallas kernels  83.3 us (45%)
  starting transfers between devices  47 us (26%)
  local copies, waits for them, and re-layouts  36.5 us (20%)
  waiting for transfers between devices  14.5 us (8%)
    pallas_call x4, Pallas kernels, advance(): call(functools.partial(step, levels, count, rows, chunks, per_chunk, rims...  49.9 us
    unnamed x62, local copies, waits for them, and re-layouts  36.5 us
    ppermute x16, starting transfers between devices, shift(): return lax.ppermute(value, axis, pairs)  31.9 us
    pallas_call x1, Pallas kernels, per_device(): call(functools.partial(soundings, levels, rows, lon_count, lat_count, cap...  16.1 us
    ppermute x16, waiting for transfers between devices, shift(): return lax.ppermute(value, axis, pairs)  14.5 us
    pallas_call x1, Pallas kernels, per_device(): call(functools.partial(first_rims, levels, tracers, rows, chunks, per_chu...  7.81 us
    pallas_call x1, Pallas kernels, per_device(): call(functools.partial(coefficients, levels, rows, per_chunk), (f32(level...  6.02 us
    all_to_all x1, starting transfers between devices, per_device(): lax.all_to_all(back.reshape(lon_count * lat_count, 1, LANES), ('lon', 'la...  5.85 us
  transfers between devices with their start and end apart: 19, of which 5 were waited for; matrix products, arithmetic and copies ran while one was open for 0% of the time, Pallas kernels for 40%

commit v1 on v0

--- a/solution.py
+++ b/solution.py
@@ -38,49 +38,60 @@
     )
 
 
+def sweep(levels, unroll, level, carry):
+    while levels % unroll:
+        unroll -= 1
+
+    def body(i, carry):
+        for u in range(unroll):
+            carry = level(i * unroll + u, carry)
+        return carry
+
+    return lax.fori_loop(0, levels // unroll, body, carry)
+
+
 def f32(*shape):
     return jax.ShapeDtypeStruct(shape, jnp.float32)
 
 
-def put_rim(value, lane, q, chunk, rows, east_ref, west_ref):
-    turned = pltpu.roll(value, 2 * q + 2, 1)
-    east_ref[chunk, rows, :] = jnp.where(lane == 2 * q + 1, turned, east_ref[chunk, rows, :])
-    if west_ref is not None:
-        west_ref[chunk, rows, :] = jnp.where(lane == 2 * q + 2, turned, west_ref[chunk, rows, :])
-
-
-def put_rows(field_ref, north_ref, south_ref, row_count, count):
+def put_rims(field, rows, levels, per_chunk, chunks, out, first, plane):
+    lane = lane_iota()
+
+    for chunk in range(chunks):
+        count = min(per_chunk, levels - chunk * per_chunk)
+
+        def body(i, carry, chunk=chunk, count=count):
+            r = pl.multiple_of(i * SUB, SUB)
+            made = jnp.zeros((SUB, LANES), jnp.float32)
+            for q in range(count):
+                at = pl.multiple_of((chunk * per_chunk + q) * plane + r, SUB)
+                turned = pltpu.roll(field[pl.ds(at, SUB), :], 2 * q + 2, 1)
+                made = jnp.where(lane >= 2 * q + 1, turned, made)
+            out[chunk, pl.ds(pl.multiple_of(first + r, SUB), SUB), :] = made
+            return carry
+
+        lax.fori_loop(0, plane // SUB, body, 0)
+
+
+def put_rows(field, north, south, rows, count):
+    unroll = next(u for u in (9, 8, 4, 2, 1) if count // SUB % u == 0)
+
     def body(i, carry):
-        start = pl.multiple_of(i * SUB, SUB)
-        first = start * row_count
-        if south_ref is not None:
-            south_ref[pl.ds(start, SUB), :] = field_ref[pl.ds(first, SUB, stride=row_count), :]
-        if north_ref is not None:
-            north_ref[pl.ds(start, SUB), :] = field_ref[
-                pl.ds(first + row_count - 1, SUB, stride=row_count), :
-            ]
+        for u in range(unroll):
+            start = pl.multiple_of((i * unroll + u) * SUB, SUB)
+            at = start * rows
+            if south is not None:
+                south[pl.ds(start, SUB), :] = field[pl.ds(at, SUB, stride=rows), :]
+            north[pl.ds(start, SUB), :] = field[pl.ds(at + rows - 1, SUB, stride=rows), :]
         return carry
 
-    lax.fori_loop(0, count // SUB, body, 0)
-
-
-def first_rims(levels, tracers, rows, chunks, per_chunk, field, east, north, e_ref, w_ref, s_ref, n_ref):
-    lane = lane_iota()
-    e_ref[...] = jnp.zeros(e_ref.shape, jnp.float32)
-    w_ref[...] = jnp.zeros(w_ref.shape, jnp.float32)
+    lax.fori_loop(0, count // SUB // unroll, body, 0)
+
+
+def first_rims(levels, tracers, rows, chunks, per_chunk, field, east, north, side, s_ref, n_ref):
     plane = tracers * rows
-    for chunk in range(chunks):
-        def body(q, carry, chunk=chunk):
-            k = chunk * per_chunk + q
-            for r in range(0, plane, SUB):
-                at = pl.multiple_of(k * plane + r, SUB)
-                put_rim(field[pl.ds(at, SUB), :], lane, q, chunk, pl.ds(r, SUB), e_ref, w_ref)
-            for r in range(0, rows, SUB):
-                at = pl.multiple_of(k * rows + r, SUB)
-                put_rim(east[pl.ds(at, SUB), :], lane, q, chunk, pl.ds(plane + r, SUB), e_ref, None)
-            return carry
-
-        lax.fori_loop(0, min(per_chunk, levels - chunk * per_chunk), body, 0)
+    put_rims(field, rows, levels, per_chunk, chunks, side, 0, plane)
+    put_rims(east, rows, levels, per_chunk, chunks, side, plane, rows)
     put_rows(field, n_ref.at[pl.ds(0, levels * tracers)], s_ref, rows, levels * tracers)
     put_rows(north, n_ref.at[pl.ds(levels * tracers, levels)], None, rows, levels)
 
@@ -90,7 +101,7 @@
     lane, sub = lane_iota(), sub_iota()
     halves = rows // SUB
 
-    def body(k, carry):
+    def level(k, carry):
         chunk, q = k // per_chunk, k % per_chunk
         has_up = (k < levels - 1).astype(jnp.float32)
         new = []
@@ -128,7 +139,7 @@
         return tuple(new)
 
     zero = jnp.zeros((SUB, LANES), jnp.float32)
-    lax.fori_loop(0, levels, body, tuple((zero, zero) for _ in range(halves)))
+    sweep(levels, 8, level, tuple((zero, zero) for _ in range(halves)))
 
 
 def step(levels, tracers, rows, chunks, per_chunk, rims_out, spread, *refs):
@@ -139,8 +150,8 @@
     base = refs.pop(0) if spread else None
     out = refs.pop(0)
     if rims_out:
-        e_ref, w_ref, s_ref, n_ref = refs[:4]
-        refs = refs[4:]
+        side_ref, s_ref, n_ref = refs[:3]
+        refs = refs[3:]
     rim = refs.pop(0)
     solved = refs.pop(0) if spread else out
     lane, sub = lane_iota(), sub_iota()
@@ -189,15 +200,11 @@
         return tuple(new)
 
     zero = jnp.zeros((SUB, LANES), jnp.float32)
-    lax.fori_loop(0, levels, forward, (zero,) * (tracers * halves))
-
-    if rims_out:
-        e_ref[...] = jnp.zeros(e_ref.shape, jnp.float32)
-        w_ref[...] = jnp.zeros(w_ref.shape, jnp.float32)
+    unroll = 2 if tracers > 1 else 8
+    sweep(levels, unroll, forward, (zero,) * (tracers * halves))
 
     def backward(i, carry):
         k = levels - 1 - i
-        chunk, q = k // per_chunk, k % per_chunk
         new = []
         for h in range(halves):
             f = above[pl.ds(pl.multiple_of(k * rows + h * SUB, SUB), SUB), :]
@@ -207,8 +214,6 @@
                 value = solved[blk, :] + f * carry[h * tracers + t]
                 if not spread:
                     out[blk, :] = value
-                if rims_out:
-                    put_rim(value, lane, q, chunk, pl.ds(r, SUB), e_ref, w_ref)
                 new.append(value)
             if spread:
                 for t in range(spread):
@@ -216,8 +221,9 @@
                     out[blk, :] = base[blk, :] + new[-1]
         return tuple(new)
 
-    lax.fori_loop(0, levels, backward, (zero,) * (tracers * halves))
+    sweep(levels, unroll, backward, (zero,) * (tracers * halves))
     if rims_out:
+        put_rims(out, rows, levels, per_chunk, chunks, side_ref, 0, plane)
         put_rows(out, n_ref, s_ref, rows, levels * tracers)
 
 
@@ -263,44 +269,57 @@
     lax.fori_loop(0, rows // SUB, body, 0)
 
 
-def tracer_sum(concentration, high, low):
+def tracer_sum(concentration, out):
     total = jnp.sum(concentration[...], axis=1)
-    total = total.reshape(total.shape[0] * total.shape[1], total.shape[2])
-    top = total.astype(jnp.bfloat16)
-    high[...] = top
-    low[...] = (total - top.astype(jnp.float32)).astype(jnp.bfloat16)
+    levels, rows, cols = total.shape
+    for h in range(rows // SUB):
+        part = total[:, h * SUB : (h + 1) * SUB, :].reshape(levels * SUB, cols)
+        top = part.astype(jnp.bfloat16)
+        lanes = pl.ds(h * cols, cols)
+        out[0, :, lanes] = top
+        out[1, :, lanes] = (part - top.astype(jnp.float32)).astype(jnp.bfloat16)
 
 
 def soundings(
-    levels, rows, lon_count, lat_count, cap, chunks, per_chunk,
-    arrived, high, low, forcing, e_ref, w_ref, s_ref, n_ref, back, table, scaled
+    levels, rows, lon_count, lat_count, cap, chunks, per_chunk, block,
+    arrived, sums, forcing, side_ref, s_ref, n_ref, back, table, scaled
 ):
     width = lon_count * cap
-    blocks = levels // SUB
-    row_index = lax.broadcasted_iota(jnp.int32, (rows, width), 0)
-    cell_index = lax.broadcasted_iota(jnp.int32, (LANES, width), 0)
-
-    def row_mask(j):
-        col = arrived[j, pl.ds(levels, 1), :].astype(jnp.int32)
-        return row_index == (col >> 7)
+    halves = rows // SUB
+    keys = halves * LANES
+    sub_index = lax.broadcasted_iota(jnp.int32, (SUB, width), 0)
+    key_index = lax.broadcasted_iota(jnp.int32, (keys, width), 0)
+    turned_index = lax.broadcasted_iota(jnp.int32, (LANES, keys), 1)
+
+    def columns(j):
+        return arrived[j, pl.ds(levels, 1), :].astype(jnp.int32)
+
+    def key_of(col):
+        return (col >> 10) * LANES + (col & (LANES - 1))
+
+    def mask_of(j):
+        return sub_index == ((columns(j) >> 7) & (SUB - 1))
 
     for j in range(lat_count):
-        col = arrived[j, pl.ds(levels, 1), :].astype(jnp.int32)
-        lookup = jnp.where(cell_index == (col & (LANES - 1)), 1.0, 0.0).astype(jnp.bfloat16)
-        table[j, :, :] = lookup
-
-        def gather(b, total, j=j):
-            blk = pl.ds(pl.multiple_of(b * SUB * rows, SUB * rows), SUB * rows)
-            look = table[j, :, :]
-            seen = jnp.dot(high[blk, :], look, preferred_element_type=jnp.float32)
-            seen += jnp.dot(low[blk, :], look, preferred_element_type=jnp.float32)
-            weight = arrived[j, pl.ds(pl.multiple_of(b * SUB, SUB), SUB), :]
-            for kk in range(SUB):
-                total += weight[kk : kk + 1, :] * seen[kk * rows : (kk + 1) * rows, :]
-            return total
-
-        total = lax.fori_loop(0, blocks, gather, jnp.zeros((rows, width), jnp.float32))
-        modelled = jnp.sum(jnp.where(row_mask(j), total, 0.0), axis=0, keepdims=True)
+        col = columns(j)
+        key = key_of(col)
+        look = jnp.where(key_index == key, 1.0, 0.0).astype(jnp.bfloat16)
+        for c in range(width // LANES):
+            piece = key[:, c * LANES : (c + 1) * LANES].astype(jnp.float32)
+            across = jnp.broadcast_to(piece, (LANES, LANES)).T.astype(jnp.int32)
+            across = jnp.concatenate([across] * halves, axis=1)
+            table[j, pl.ds(c * LANES, LANES), :] = jnp.where(turned_index == across, 1.0, 0.0).astype(
+                jnp.bfloat16
+            )
+        total = jnp.zeros((SUB, width), jnp.float32)
+        for b in range(levels // block):
+            blk = pl.ds(b * block * SUB, block * SUB)
+            seen = jnp.dot(sums[0, blk, :], look, preferred_element_type=jnp.float32)
+            seen += jnp.dot(sums[1, blk, :], look, preferred_element_type=jnp.float32)
+            weight = arrived[j, pl.ds(b * block, block), :]
+            for k in range(block):
+                total += weight[k : k + 1, :] * seen[k * SUB : (k + 1) * SUB, :]
+        modelled = jnp.sum(jnp.where(mask_of(j), total, 0.0), axis=0, keepdims=True)
         observed = arrived[j, pl.ds(levels + 1, 1), :]
         error = arrived[j, pl.ds(levels + 2, 1), :]
         residual = jnp.where(col >= 0, (modelled - observed) / error, 0.0)
@@ -312,35 +331,24 @@
                 piece = pltpu.roll(piece, LANES - at % LANES, 1)
             back[pl.ds(i * lat_count + j, 1), :] = piece
 
-    def scatter(b, carry):
-        total = jnp.zeros((SUB * rows, LANES), jnp.float32)
+    for b in range(levels // block):
+        total = jnp.zeros((block * SUB, keys), jnp.float32)
         for j in range(lat_count):
-            weight = arrived[j, pl.ds(pl.multiple_of(b * SUB, SUB), SUB), :] * scaled[pl.ds(j, 1), :]
+            weight = arrived[j, pl.ds(b * block, block), :] * scaled[pl.ds(j, 1), :]
             top = weight.astype(jnp.bfloat16).astype(jnp.float32)
-            mask = row_mask(j)
+            mask = mask_of(j)
             for part in (top, weight - top):
                 spread = jnp.concatenate(
-                    [jnp.where(mask, part[kk : kk + 1, :], 0.0) for kk in range(SUB)], axis=0
+                    [jnp.where(mask, part[k : k + 1, :], 0.0) for k in range(block)], axis=0
                 ).astype(jnp.bfloat16)
-                total += lax.dot_general(
-                    spread, table[j, :, :], (((1,), (1,)), ((), ())), preferred_element_type=jnp.float32
-                )
-        forcing[pl.ds(pl.multiple_of(b * SUB * rows, SUB * rows), SUB * rows), :] = total
-        return carry
-
-    lax.fori_loop(0, blocks, scatter, 0)
-
-    lane = lane_iota()
-    e_ref[...] = jnp.zeros(e_ref.shape, jnp.float32)
-    w_ref[...] = jnp.zeros(w_ref.shape, jnp.float32)
-    for chunk in range(chunks):
-        def body(q, carry, chunk=chunk):
-            for r in range(0, rows, SUB):
-                at = pl.multiple_of((chunk * per_chunk + q) * rows + r, SUB)
-                put_rim(forcing[pl.ds(at, SUB), :], lane, q, chunk, pl.ds(r, SUB), e_ref, w_ref)
-            return carry
-
-        lax.fori_loop(0, min(per_chunk, levels - chunk * per_chunk), body, 0)
+                total += jnp.dot(spread, table[j, :, :], preferred_element_type=jnp.float32)
+        for k in range(block):
+            for h in range(halves):
+                forcing[pl.ds((b * block + k) * rows + h * SUB, SUB), :] = total[
+                    k * SUB : (k + 1) * SUB, h * LANES : (h + 1) * LANES
+                ]
+
+    put_rims(forcing, rows, levels, per_chunk, chunks, side_ref, 0, rows)
     put_rows(forcing, n_ref, s_ref, rows, levels)
 
 
@@ -366,10 +374,10 @@
     return lax.ppermute(value, axis, pairs)
 
 
-def exchange(east_rim, west_rim, south_rim, north_rim):
+def exchange(side_rim, south_rim, north_rim):
     return (
-        shift(east_rim, "lon", 1, True),
-        shift(west_rim, "lon", -1, True),
+        shift(side_rim, "lon", 1, True),
+        shift(side_rim, "lon", -1, True),
         shift(south_rim, "lat", -1, False),
         shift(north_rim, "lat", 1, False),
     )
@@ -393,7 +401,7 @@
 
     packed = call(
         functools.partial(pack, levels, lon_count),
-        f32(lon_count, sent_rows, lat_count * cap), (), 8, 10, 800000, "pack",
+        f32(lon_count, sent_rows, lat_count * cap), (), 2, 10, 800000, "pack",
     )(flat(kernel), flat(sound_col), flat(observed), flat(obs_error))
     by_lon = lax.all_to_all(packed, "lon", split_axis=0, concat_axis=0, tiled=True)
 
@@ -402,36 +410,28 @@
     rims = call(
         functools.partial(first_rims, levels, tracers, rows, chunks, per_chunk),
         (
-            f32(chunks, plane + rows, LANES), f32(chunks, plane, LANES),
+            f32(chunks, plane + rows, LANES),
             f32(levels * tracers, LANES), f32(levels * tracers + levels, LANES),
         ),
-        (), 16, field_bytes, 2 * field_bytes, "first_rims",
+        (), 2, field_bytes, 2 * field_bytes, "first_rims",
     )(field, east, north)
     from_west, from_east, from_north, from_south = exchange(*rims)
 
     by_lat = call(
         functools.partial(repack, sent_rows, lon_count, lat_count, cap),
-        f32(lat_count, sent_rows, lon_count * cap), (), 8, 10, 800000, "repack",
+        f32(lat_count, sent_rows, lon_count * cap), (), 2, 10, 800000, "repack",
     )(by_lon)
     arrived = lax.all_to_all(by_lat, "lat", split_axis=0, concat_axis=0, tiled=True)
 
-    level_block = SUB
-    high, low = pl.pallas_call(
+    sums = call(
         tracer_sum,
-        grid=(levels // level_block,),
-        in_specs=[pl.BlockSpec((level_block, tracers, rows, cols), lambda i: (i, 0, 0, 0))],
-        out_specs=[pl.BlockSpec((level_block * rows, cols), lambda i: (i, 0))] * 2,
-        out_shape=[jax.ShapeDtypeStruct((levels * rows, cols), jnp.bfloat16)] * 2,
-        compiler_params=pltpu.CompilerParams(vmem_limit_bytes=8 * MIB),
-        cost_estimate=pl.CostEstimate(
-            flops=field_bytes // 4, bytes_accessed=field_bytes, transcendentals=0
-        ),
-        name="tracer_sum",
+        jax.ShapeDtypeStruct((2, levels * SUB, rows // SUB * cols), jnp.bfloat16),
+        (), 4, field_bytes // 4, field_bytes, "tracer_sum",
     )(concentration)
 
     weights = call(
         functools.partial(coefficients, levels, rows, per_chunk),
-        (f32(levels * rows, LANES),) * 7, (), 12, field_bytes * 2, field_bytes * 2, "coefficients",
+        (f32(levels * rows, LANES),) * 7, (), 2, field_bytes * 2, field_bytes * 2, "coefficients",
     )(
         east, north, mix,
         lax.slice_in_dim(from_west, plane, plane + rows, axis=1),
@@ -440,7 +440,7 @@
 
     def rim_shapes(count):
         return (
-            f32(chunks, count * rows, LANES), f32(chunks, count * rows, LANES),
+            f32(chunks, count * rows, LANES),
             f32(levels * count, LANES), f32(levels * count, LANES),
         )
 
@@ -453,23 +453,24 @@
         return call(
             functools.partial(step, levels, count, rows, chunks, per_chunk, rims_out, spread),
             (out,) + rim_shapes(count) if rims_out else out,
-            scratch, 24, field_bytes * count, field_bytes * count // 2 + 4 * field_bytes // 8 * bool(spread),
+            scratch, 8 if spread else 2, field_bytes * count, field_bytes * count // 2 + 4 * field_bytes // 8 * bool(spread),
             "step",
         )(value, *rims, *weights, *(() if base is None else (base,)))
 
     stepped, *rims = advance(field, (from_west, from_east, from_north, from_south), tracers, True)
     finished = advance(stepped, exchange(*rims), tracers, False)
 
+    block = next(u for u in (24, 16, 8) if levels % u == 0)
     forcing, *rest = call(
-        functools.partial(soundings, levels, rows, lon_count, lat_count, cap, chunks, per_chunk),
+        functools.partial(soundings, levels, rows, lon_count, lat_count, cap, chunks, per_chunk, block),
         (f32(levels * rows, LANES),) + rim_shapes(1) + (f32(lon_count * lat_count, LANES),),
         (
-            pltpu.VMEM((lat_count, LANES, lon_count * cap), jnp.bfloat16),
+            pltpu.VMEM((lat_count, lon_count * cap, rows // SUB * LANES), jnp.bfloat16),
             pltpu.VMEM((max(lat_count, SUB), lon_count * cap), jnp.float32),
         ),
-        16, field_bytes * 8, field_bytes, "soundings",
-    )(arrived, high, low)
-    rims, back = rest[:4], rest[4]
+        8, field_bytes * 8, field_bytes, "soundings",
+    )(arrived, sums)
+    rims, back = rest[:3], rest[3]
     stepped_forcing, *rims = advance(forcing, exchange(*rims), 1, True)
 
     returned = lax.all_to_all(
@@ -478,7 +479,7 @@
     )
     residual = call(
         functools.partial(unpack, lon_count, lat_count, cap),
-        f32(per_level, LANES), (), 4, 10, 10000, "unpack",
+        f32(per_level, LANES), (), 2, 10, 10000, "unpack",
     )(returned.reshape(lon_count * lat_count, LANES))
 
     result = advance(stepped_forcing, exchange(*rims), 1, False, finished)

time: 184 us -> 138 us (0.75)
  Pallas kernels: 83.3 us -> 39.9 us
  local copies, waits for them, and re-layouts: 36.5 us -> 33.7 us
  waiting for transfers between devices: 14.5 us -> 17.1 us
    pallas_call x4, Pallas kernels: 49.9 us -> 27.1 us  [advance(): call(functools.partial(step, levels, count, rows, chunks, per_chunk, rims...]
    pallas_call x1, Pallas kernels: 16.1 us -> 3.13 us  [per_device(): call(functools.partial(soundings, levels, rows, lon_count, lat_count, cap...]
    pallas_call x1, Pallas kernels: 6.02 us -> 1.38 us  [per_device(): call(functools.partial(coefficients, levels, rows, per_chunk), (f32(level...]
    pallas_call x1, Pallas kernels: 7.81 us -> 4.82 us  [per_device(): call(functools.partial(first_rims, levels, tracers, rows, chunks, per_chu...]
    unnamed x62 -> x56, local copies, waits for them, and re-layouts: 36.5 us -> 33.7 us
    ppermute x16, waiting for transfers between devices: 14.5 us -> 17.1 us  [shift(): return lax.ppermute(value, axis, pairs)]
  transfers between devices with their start and end apart: 19 -> 19, of which waited for: 5 -> 6; matrix products, arithmetic and copies ran while one was open for 0% -> 0% of each run, Pallas kernels for 40% -> 25%
where the time goes in v1:
time: 138 us; the launch traced here: 137 us
  starting transfers between devices  45.2 us (33%)
  Pallas kernels  39.9 us (29%)
  local copies, waits for them, and re-layouts  33.7 us (24%)
  waiting for transfers between devices  17.1 us (12%)
    unnamed x56, local copies, waits for them, and re-layouts  33.7 us
    ppermute x16, starting transfers between devices, shift(): return lax.ppermute(value, axis, pairs)  31.8 us
    pallas_call x4, Pallas kernels, advance(): call(functools.partial(step, levels, count, rows, chunks, per_chunk, rims...  27.1 us
    ppermute x16, waiting for transfers between devices, shift(): return lax.ppermute(value, axis, pairs)  17.1 us
    all_to_all x1, starting transfers between devices, per_device(): lax.all_to_all(packed, 'lon', split_axis=0, concat_axis=0, tiled=True)  5.17 us
    pallas_call x1, Pallas kernels, per_device(): call(functools.partial(first_rims, levels, tracers, rows, chunks, per_chu...  4.82 us
    all_to_all x1, starting transfers between devices, per_device(): lax.all_to_all(back.reshape(lon_count * lat_count, 1, LANES), ('lon', 'la...  4.13 us
    all_to_all x1, starting transfers between devices, per_device(): lax.all_to_all(by_lat, 'lat', split_axis=0, concat_axis=0, tiled=True)  4.1 us
  transfers between devices with their start and end apart: 19, of which 6 were waited for; matrix products, arithmetic and copies ran while one was open for 0% of the time, Pallas kernels for 25%

profile of v1, /device:TPU:0, one launch (start us, length us, event | category | flops | bytes accessed | tf_op | source)
XLA Modules:
  0.0 136.7 jit_solution(17082663673286453664)
XLA Ops:
  0.6 1.0 copy-done.22
  1.6 0.7 copy-done.24
  2.3 0.7 copy-done.25
  3.0 0.7 copy-done.26
  3.7 0.8 pack.1
  4.4 5.2 %all-to-all-start = ((f32[8,80,128]{2,1,0:T(8,128)}), f32[8,80,128]{2,1,0:T(8,128)S(1)}, u32[]{:S(2)}, u32[]{:S(2)}) async-start(f32[8,80,128]{2,1,0:T(8,128)} %pack.1), calls=%async_computation | async-start | bytes 655360 | tf_op jit(solution)/shard_map/all_to_all | solution.py:406
  9.6 2.3 %copy-done.2 = f32[72,8,16,128]{3,2,1,0:T(8,128)S(1)} copy-done((f32[72,8,16,128]{3,2,1,0:T(8,128)S(1)}, f32[72,8,16,128]{3,2,1,0:T(8,128)}, u32[]{:S(2)}) %copy-start.2) | copy-done | bytes 4718616
  11.9 1.1 copy-done.11
  13.0 1.1 copy-done.13
  14.1 4.8 %first_rims.1 = (f32[2,144,128]{2,1,0:T(8,128)}, f32[576,128]{1,0:T(8,128)}, f32[648,128]{1,0:T(8,128)S(1)}) custom-call(f32[9216,128]{1,0:T(8,128)S(1)} %bitcast.14, f32[1152,128]{1,0:T(8,128)S(1)} %bitcast.16, f32[1152,128]{1,0:T(8,128)S(1)} %bitcast.18), custom_call_target="tpu_custom_call" | custom-call | flops 4718592 | bytes 9437184 | tf_op jit(solution)/shard_map/first_rims/pallas_call | solution.py:410
  18.9 3.5 %collective-permute-start.5 = (f32[648,128]{1,0:T(8,128)S(1)}, f32[648,128]{1,0:T(8,128)S(1)}, u32[]{:S(2)}, u32[]{:S(2)}) collective-permute-start(f32[648,128]{1,0:T(8,128)S(1)} %get-tuple-element.30), channel_id=1, source_target_pairs={{0,1},{1,2},{2,3},{4,5},{5,6},{6,7},{8,9},{9,10},{10,11},{12,13},{... | collective-permute-start | bytes 995336 | tf_op jit(solution)/shard_map/ppermute | solution.py:374
  22.4 0.0 all-to-all-done.arrived
  22.4 1.7 %repack.1 = f32[4,80,256]{2,1,0:T(8,128)} custom-call(f32[8,80,128]{2,1,0:T(8,128)S(1)} %all-to-all-done.arrived), custom_call_target="tpu_custom_call" | custom-call | flops 10 | bytes 800000 | tf_op jit(solution)/shard_map/repack/pallas_call | solution.py:420
  24.1 4.1 %all-to-all-start.1 = ((f32[4,80,256]{2,1,0:T(8,128)}), f32[4,80,256]{2,1,0:T(8,128)}, u32[]{:S(2)}, u32[]{:S(2)}) async-start(f32[4,80,256]{2,1,0:T(8,128)} %repack.1), calls=%async_computation.1 | async-start | bytes 655360 | tf_op jit(solution)/shard_map/all_to_all | solution.py:424
  28.2 1.3 collective-permute-start.11
  29.5 0.3 collective-permute-start.4
  29.8 2.4 %collective-permute-start.10 = (f32[2,144,128]{2,1,0:T(8,128)}, f32[2,144,128]{2,1,0:T(8,128)S(1)}, u32[]{:S(2)}, u32[]{:S(2)}) collective-permute-start(f32[2,144,128]{2,1,0:T(8,128)} %get-tuple-element.29), channel_id=1, source_target_pairs={{0,28},{4,0},{8,4},{12,8},{16,12},{20,16},{24,20},{28,24},{1,29},{... | collective-permute-start | bytes 442376 | tf_op jit(solution)/shard_map/ppermute | solution.py:374
  32.2 3.0 %collective-permute-done.4.refs_1_ = f32[2,144,128]{2,1,0:T(8,128)S(1)} collective-permute-done((f32[2,144,128]{2,1,0:T(8,128)}, f32[2,144,128]{2,1,0:T(8,128)S(1)}, u32[]{:S(2)}, u32[]{:S(2)}) %collective-permute-start.4) | collective-permute-done | bytes 147488 | tf_op jit(solution)/shard_map/ppermute | solution.py:374
  35.2 0.0 copy-start.20
  35.2 0.7 copy-done.20
  35.9 1.1 copy-done.12
  37.0 1.1 copy-done.14
  38.1 1.1 copy-done.19
  39.1 1.4 %coefficients.1 = (f32[1152,128]{1,0:T(8,128)S(1)}, f32[1152,128]{1,0:T(8,128)S(1)}, f32[1152,128]{1,0:T(8,128)S(1)}, f32[1152,128]{1,0:T(8,128)S(1)}, f32[1152,...) custom-call(f32[1152,128]{1,0:T(8,128)S(1)} %bitcast.17, f32[1152,128]{1,0:T(8,128)S(1)} %bitcast.19, ...), custom_call_target="tpu_custom_call" | custom-call | flops 9437184 | bytes 9437184 | tf_op jit(solution)/shard_map/coefficients/pallas_call | solution.py:432
  40.5 2.3 %collective-permute-done.11.refs_3_ = f32[576,128]{1,0:T(8,128)S(1)} collective-permute-done((f32[576,128]{1,0:T(8,128)}, f32[576,128]{1,0:T(8,128)S(1)}, u32[]{:S(2)}, u32[]{:S(2)}) %collective-permute-start.11) | collective-permute-done | bytes 294944 | tf_op jit(solution)/shard_map/ppermute | solution.py:374
  42.9 2.3 %copy-done.3 = f32[72,8,16,128]{3,2,1,0:T(8,128)S(1)} copy-done((f32[72,8,16,128]{3,2,1,0:T(8,128)S(1)}, f32[72,8,16,128]{3,2,1,0:T(8,128)}, u32[]{:S(2)}) %copy-start.3) | copy-done | bytes 4718616
  45.2 1.0 copy-done.21
  46.2 11.5 %step.5 = (f32[9216,128]{1,0:T(8,128)S(1)}, f32[2,128,128]{2,1,0:T(8,128)}, f32[576,128]{1,0:T(8,128)}, f32[576,128]{1,0:T(8,128)}) custom-call(f32[9216,128]{1,0:T(8,128)S(1)} %bitcast.15, f32[2,144,128]{2,1,0:T(8,128)S(1)} %collective-permute-done.4.refs_1_, f32[2,144,128]{2,1,0:T(8,128)S(1)} %collective-permute-done.10.refs_2_, ...), custom_call_target="tpu_custom_call" | custom-call | flops 37748736 | bytes 18874368 | tf_op jit(solution)/shard_map/step/pallas_call | solution.py:453
  57.7 2.2 %copy-done.8 = f32[9216,128]{1,0:T(8,128)} copy-done((f32[9216,128]{1,0:T(8,128)}, f32[9216,128]{1,0:T(8,128)S(1)}, u32[]{:S(2)}) %copy-start.8) | copy-done | bytes 4718616
  59.9 1.3 collective-permute-start.14
  61.2 6.3 %collective-permute-start.15 = (f32[576,128]{1,0:T(8,128)}, f32[576,128]{1,0:T(8,128)}, u32[]{:S(2)}, u32[]{:S(2)}) collective-permute-start(f32[576,128]{1,0:T(8,128)} %get-tuple-element.46), channel_id=1, source_target_pairs={{0,1},{1,2},{2,3},{4,5},{5,6},{6,7},{8,9},{9,10},{10,11},{12,13},{... | collective-permute-start | bytes 884744 | tf_op jit(solution)/shard_map/ppermute | solution.py:374
  67.6 2.3 %copy-done.10 = f32[72,8,16,128]{3,2,1,0:T(8,128)S(1)} copy-done((f32[72,8,16,128]{3,2,1,0:T(8,128)S(1)}, f32[72,8,16,128]{3,2,1,0:T(8,128)}, u32[]{:S(2)}) %copy-start.10) | copy-done | bytes 4718616
  69.9 0.3 tracer_sum.1.sums
  70.2 0.8 copy-done.15
  71.1 2.6 %collective-permute-start.13 = (f32[2,128,128]{2,1,0:T(8,128)}, f32[2,128,128]{2,1,0:T(8,128)}, u32[]{:S(2)}, u32[]{:S(2)}) collective-permute-start(f32[2,128,128]{2,1,0:T(8,128)} %get-tuple-element.44), channel_id=1, source_target_pairs={{0,28},{4,0},{8,4},{12,8},{16,12},{20,16},{24,20},{28,24},{1,29},{... | collective-permute-start | bytes 393224 | tf_op jit(solution)/shard_map/ppermute | solution.py:374
  73.7 1.1 copy-done.16
  74.8 3.1 %soundings.1 = (f32[1152,128]{1,0:T(8,128)S(1)}, f32[2,16,128]{2,1,0:T(8,128)S(1)}, f32[72,128]{1,0:T(8,128)S(1)}, f32[72,128]{1,0:T(8,128)S(1)}, f32[32,128]{1,0:T(8,128)S(1)}) custom-call(f32[4,80,256]{2,1,0:T(8,128)} %all-to-all-done.1.arrived, bf16[2,576,256]{2,1,0:T(8,128)(2,1)S(1)} %copy-done.16), custom_call_target="tpu_custom_call" | custom-call | flops 37748736 | bytes 4718592 | tf_op jit(solution)/shard_map/soundings/pallas_call | solution.py:464
  78.0 0.1 collective-permute-start
  78.0 4.0 %collective-permute-done.refs_1_ = f32[2,16,128]{2,1,0:T(8,128)S(1)} collective-permute-done((f32[2,16,128]{2,1,0:T(8,128)S(1)}, f32[2,16,128]{2,1,0:T(8,128)S(1)}, u32[]{:S(2)}, u32[]{:S(2)}) %collective-permute-start) | collective-permute-done | bytes 16416 | tf_op jit(solution)/shard_map/ppermute | solution.py:374
  82.1 1.4 %collective-permute-done.1.refs_2_ = f32[2,16,128]{2,1,0:T(8,128)S(1)} collective-permute-done((f32[2,16,128]{2,1,0:T(8,128)S(1)}, f32[2,16,128]{2,1,0:T(8,128)S(1)}, u32[]{:S(2)}, u32[]{:S(2)}) %collective-permute-start.1) | collective-permute-done | bytes 16416 | tf_op jit(solution)/shard_map/ppermute | solution.py:374
  83.5 1.3 collective-permute-start.2
  84.8 4.6 %collective-permute-done.2.refs_3_ = f32[72,128]{1,0:T(8,128)S(1)} collective-permute-done((f32[72,128]{1,0:T(8,128)S(1)}, f32[72,128]{1,0:T(8,128)S(1)}, u32[]{:S(2)}, u32[]{:S(2)}) %collective-permute-start.2) | collective-permute-done | bytes 36896 | tf_op jit(solution)/shard_map/ppermute | solution.py:374
  89.4 3.2 %collective-permute-start.3 = (f32[72,128]{1,0:T(8,128)S(1)}, f32[72,128]{1,0:T(8,128)S(1)}, u32[]{:S(2)}, u32[]{:S(2)}) collective-permute-start(f32[72,128]{1,0:T(8,128)S(1)} %get-tuple-element.28), channel_id=1, source_target_pairs={{0,1},{1,2},{2,3},{4,5},{5,6},{6,7},{8,9},{9,10},{10,11},{12,13},{... | collective-permute-start | bytes 110600 | tf_op jit(solution)/shard_map/ppermute | solution.py:374
  92.6 1.6 %collective-permute-done.3.refs_4_ = f32[72,128]{1,0:T(8,128)S(1)} collective-permute-done((f32[72,128]{1,0:T(8,128)S(1)}, f32[72,128]{1,0:T(8,128)S(1)}, u32[]{:S(2)}, u32[]{:S(2)}) %collective-permute-start.3) | collective-permute-done | bytes 36896 | tf_op jit(solution)/shard_map/ppermute | solution.py:374
  94.2 1.1 copy-done.5
  95.3 2.6 %step.4 = (f32[1152,128]{1,0:T(8,128)S(1)}, f32[2,16,128]{2,1,0:T(8,128)S(1)}, f32[72,128]{1,0:T(8,128)}, f32[72,128]{1,0:T(8,128)}) custom-call(f32[1152,128]{1,0:T(8,128)S(1)} %get-tuple-element.25.refs_0_, f32[2,16,128]{2,1,0:T(8,128)S(1)} %collective-permute-done.refs_1_, f32[2,16,128]{2,1,0:T(8,128)S(1)} %collective-permute-done.1.refs_2_, ...), custom_call_target="tpu_custom_call" | custom-call | flops 4718592 | bytes 2359296 | tf_op jit(solution)/shard_map/step/pallas_call | solution.py:453
  97.8 0.9 copy-done.17
  98.7 0.6 copy-done.27
  99.3 1.3 collective-permute-start.8
  100.6 5.5 %collective-permute-start.9 = (f32[72,128]{1,0:T(8,128)}, f32[72,128]{1,0:T(8,128)}, u32[]{:S(2)}, u32[]{:S(2)}) collective-permute-start(f32[72,128]{1,0:T(8,128)} %get-tuple-element.41), channel_id=1, source_target_pairs={{0,1},{1,2},{2,3},{4,5},{5,6},{6,7},{8,9},{9,10},{10,11},{12,13},{... | collective-permute-start | bytes 110600 | tf_op jit(solution)/shard_map/ppermute | solution.py:374
  106.1 4.1 %all-to-all-start.2 = ((f32[32,1,128]{2,1,0:T(1,128)}), f32[32,1,128]{2,1,0:T(1,128)S(1)}, u32[]{:S(2)}, u32[]{:S(2)}) async-start(f32[32,1,128]{2,1,0:T(1,128)} %bitcast.23), calls=%async_computation.2 | async-start | bytes 32768 | tf_op jit(solution)/shard_map/all_to_all | solution.py:476
  110.2 0.3 collective-permute-start.6
  110.5 2.4 %collective-permute-start.7 = (f32[2,16,128]{2,1,0:T(8,128)}, f32[2,16,128]{2,1,0:T(8,128)}, u32[]{:S(2)}, u32[]{:S(2)}) collective-permute-start(f32[2,16,128]{2,1,0:T(8,128)} %copy-done.27), channel_id=1, source_target_pairs={{0,28},{4,0},{8,4},{12,8},{16,12},{20,16},{24,20},{28,24},{1,29},{... | collective-permute-start | bytes 49160 | tf_op jit(solution)/shard_map/ppermute | solution.py:374
  112.9 1.1 copy-done.6
  114.0 2.3 %copy-done.9 = f32[9216,128]{1,0:T(8,128)S(1)} copy-done((f32[9216,128]{1,0:T(8,128)S(1)}, f32[9216,128]{1,0:T(8,128)}, u32[]{:S(2)}) %copy-start.9) | copy-done | bytes 4718616
  116.3 8.3 %step.6.refs_12_ = f32[9216,128]{1,0:T(8,128)S(1)} custom-call(f32[9216,128]{1,0:T(8,128)S(1)} %copy-done.9, f32[2,128,128]{2,1,0:T(8,128)} %collective-permute-done.12.refs_1_, f32[2,128,128]{2,1,0:T(8,128)} %collective-permute-done.13.refs_2_, f32[576,128]{1,0:T(8,128)} %collective-permute-done.14.refs_3_, f32[576,128]{1,0:T(8,128)} %collective-permute-done.15.refs_4_, ...), custom_call_target="tpu_custom_call" | custom-call | flops 37748736 | bytes 18874368 | tf_op jit(solution)/shard_map/step/pallas_call | solution.py:453
  124.6 0.0 copy-start
  124.6 2.2 %copy-done = f32[9216,128]{1,0:T(8,128)} copy-done((f32[9216,128]{1,0:T(8,128)}, f32[9216,128]{1,0:T(8,128)S(1)}, u32[]{:S(2)}) %copy-start) | copy-done | bytes 4718616
  126.8 0.7 unpack.1
  127.5 0.0 copy-start.1
  127.5 2.3 %copy-done.1 = f32[9216,128]{1,0:T(8,128)S(1)} copy-done((f32[9216,128]{1,0:T(8,128)S(1)}, f32[9216,128]{1,0:T(8,128)}, u32[]{:S(2)}) %copy-start.1) | copy-done | bytes 4718616
  129.8 1.1 copy-done.7
  130.9 1.1 copy-done.18
  132.0 4.7 %step.7 = f32[9216,128]{1,0:T(8,128)} custom-call(f32[1152,128]{1,0:T(8,128)S(1)} %copy-done.18, f32[2,16,128]{2,1,0:T(8,128)} %collective-permute-done.6.refs_1_, f32[2,16,128]{2,1,0:T(8,128)} %collective-permute-done.7.refs_2_, f32[72,128]{1,0:T(8,128)} %collective-permute-done.8.refs_3_, f32[72,128]{1,0:T(8,128)} %collective-permute-done.9.refs_4_, ...), custom_call_target="tpu_custom_call" | custom-call | flops 4718592 | bytes 4718592 | tf_op jit(solution)/shard_map/step/pallas_call | solution.py:453
  (43 shorter events, 0.1 us)
Async XLA Ops:
  0.6 1.0 copy-start.22
  1.6 0.7 copy-start.24
  2.3 0.7 copy-start.25
  3.0 0.7 copy-start.26
  4.4 18.0 %all-to-all-start = ((f32[8,80,128]{2,1,0:T(8,128)}), f32[8,80,128]{2,1,0:T(8,128)S(1)}, u32[]{:S(2)}, u32[]{:S(2)}) async-start(f32[8,80,128]{2,1,0:T(8,128)} %pack.1), calls=%async_computation | async-start | bytes 655360 | tf_op jit(solution)/shard_map/all_to_all | solution.py:406
  9.6 2.3 %copy-start.2 = (f32[72,8,16,128]{3,2,1,0:T(8,128)S(1)}, f32[72,8,16,128]{3,2,1,0:T(8,128)}, u32[]{:S(2)}) copy-start(f32[72,8,16,128]{3,2,1,0:T(8,128)} %param.10) | copy-start | bytes 14155780
  11.9 1.1 copy-start.11
  13.0 1.1 copy-start.13
  18.9 16.3 %collective-permute-start.5 = (f32[648,128]{1,0:T(8,128)S(1)}, f32[648,128]{1,0:T(8,128)S(1)}, u32[]{:S(2)}, u32[]{:S(2)}) collective-permute-start(f32[648,128]{1,0:T(8,128)S(1)} %get-tuple-element.30), channel_id=1, source_target_pairs={{0,1},{1,2},{2,3},{4,5},{5,6},{6,7},{8,9},{9,10},{10,11},{12,13},{... | collective-permute-start | bytes 995336 | tf_op jit(solution)/shard_map/ppermute | solution.py:374
  24.1 49.7 %all-to-all-start.1 = ((f32[4,80,256]{2,1,0:T(8,128)}), f32[4,80,256]{2,1,0:T(8,128)}, u32[]{:S(2)}, u32[]{:S(2)}) async-start(f32[4,80,256]{2,1,0:T(8,128)} %repack.1), calls=%async_computation.1 | async-start | bytes 655360 | tf_op jit(solution)/shard_map/all_to_all | solution.py:424
  28.2 14.7 %collective-permute-start.11 = (f32[576,128]{1,0:T(8,128)}, f32[576,128]{1,0:T(8,128)S(1)}, u32[]{:S(2)}, u32[]{:S(2)}) collective-permute-start(f32[576,128]{1,0:T(8,128)} %get-tuple-element.42), channel_id=1, source_target_pairs={{1,0},{2,1},{3,2},{5,4},{6,5},{7,6},{9,8},{10,9},{11,10},{13,12},{... | collective-permute-start | bytes 884744 | tf_op jit(solution)/shard_map/ppermute | solution.py:374
  29.5 5.7 %collective-permute-start.4 = (f32[2,144,128]{2,1,0:T(8,128)}, f32[2,144,128]{2,1,0:T(8,128)S(1)}, u32[]{:S(2)}, u32[]{:S(2)}) collective-permute-start(f32[2,144,128]{2,1,0:T(8,128)} %get-tuple-element.29), channel_id=1, source_target_pairs={{0,4},{4,8},{8,12},{12,16},{16,20},{20,24},{24,28},{28,0},{1,5},{5... | collective-permute-start | bytes 442376 | tf_op jit(solution)/shard_map/ppermute | solution.py:374
  29.8 10.8 %collective-permute-start.10 = (f32[2,144,128]{2,1,0:T(8,128)}, f32[2,144,128]{2,1,0:T(8,128)S(1)}, u32[]{:S(2)}, u32[]{:S(2)}) collective-permute-start(f32[2,144,128]{2,1,0:T(8,128)} %get-tuple-element.29), channel_id=1, source_target_pairs={{0,28},{4,0},{8,4},{12,8},{16,12},{20,16},{24,20},{28,24},{1,29},{... | collective-permute-start | bytes 442376 | tf_op jit(solution)/shard_map/ppermute | solution.py:374
  35.2 0.7 copy-start.20
  35.9 1.1 copy-start.12
  37.0 1.1 copy-start.14
  38.1 1.1 copy-start.19
  40.5 17.2 %copy-start.4 = (f32[1152,128]{1,0:T(8,128)}, f32[1152,128]{1,0:T(8,128)S(1)}, u32[]{:S(2)}) copy-start(f32[1152,128]{1,0:T(8,128)S(1)} %get-tuple-element.37.refs_11_) | copy-start | bytes 1769476
  42.9 2.3 %copy-start.3 = (f32[72,8,16,128]{3,2,1,0:T(8,128)S(1)}, f32[72,8,16,128]{3,2,1,0:T(8,128)}, u32[]{:S(2)}) copy-start(f32[72,8,16,128]{3,2,1,0:T(8,128)} %param.10) | copy-start | bytes 14155780
  45.2 1.0 copy-start.21
  57.7 2.2 %copy-start.8 = (f32[9216,128]{1,0:T(8,128)}, f32[9216,128]{1,0:T(8,128)S(1)}, u32[]{:S(2)}) copy-start(f32[9216,128]{1,0:T(8,128)S(1)} %get-tuple-element.43.refs_0_) | copy-start | bytes 14155780
  59.9 50.6 %collective-permute-start.14 = (f32[576,128]{1,0:T(8,128)}, f32[576,128]{1,0:T(8,128)}, u32[]{:S(2)}, u32[]{:S(2)}) collective-permute-start(f32[576,128]{1,0:T(8,128)} %get-tuple-element.45), channel_id=1, source_target_pairs={{1,0},{2,1},{3,2},{5,4},{6,5},{7,6},{9,8},{10,9},{11,10},{13,12},{... | collective-permute-start | bytes 884744 | tf_op jit(solution)/shard_map/ppermute | solution.py:374
  61.2 51.7 %collective-permute-start.15 = (f32[576,128]{1,0:T(8,128)}, f32[576,128]{1,0:T(8,128)}, u32[]{:S(2)}, u32[]{:S(2)}) collective-permute-start(f32[576,128]{1,0:T(8,128)} %get-tuple-element.46), channel_id=1, source_target_pairs={{0,1},{1,2},{2,3},{4,5},{5,6},{6,7},{8,9},{9,10},{10,11},{12,13},{... | collective-permute-start | bytes 884744 | tf_op jit(solution)/shard_map/ppermute | solution.py:374
  67.5 33.0 %collective-permute-start.12 = (f32[2,128,128]{2,1,0:T(8,128)}, f32[2,128,128]{2,1,0:T(8,128)}, u32[]{:S(2)}, u32[]{:S(2)}) collective-permute-start(f32[2,128,128]{2,1,0:T(8,128)} %get-tuple-element.44), channel_id=1, source_target_pairs={{0,4},{4,8},{8,12},{12,16},{16,20},{20,24},{24,28},{28,0},{1,5},{5... | collective-permute-start | bytes 393224 | tf_op jit(solution)/shard_map/ppermute | solution.py:374
  67.6 2.3 %copy-start.10 = (f32[72,8,16,128]{3,2,1,0:T(8,128)S(1)}, f32[72,8,16,128]{3,2,1,0:T(8,128)}, u32[]{:S(2)}) copy-start(f32[72,8,16,128]{3,2,1,0:T(8,128)} %concentration.1) | copy-start | bytes 14155780
  70.2 0.9 copy-start.15
  71.1 39.1 %collective-permute-start.13 = (f32[2,128,128]{2,1,0:T(8,128)}, f32[2,128,128]{2,1,0:T(8,128)}, u32[]{:S(2)}, u32[]{:S(2)}) collective-permute-start(f32[2,128,128]{2,1,0:T(8,128)} %get-tuple-element.44), channel_id=1, source_target_pairs={{0,28},{4,0},{8,4},{12,8},{16,12},{20,16},{24,20},{28,24},{1,29},{... | collective-permute-start | bytes 393224 | tf_op jit(solution)/shard_map/ppermute | solution.py:374
  73.7 1.1 copy-start.16
  77.9 28.1 %copy-start.23 = (f32[32,128]{1,0:T(8,128)}, f32[32,128]{1,0:T(8,128)S(1)}, u32[]{:S(2)}) copy-start(f32[32,128]{1,0:T(8,128)S(1)} %get-tuple-element.47) | copy-start | bytes 49156
  78.0 4.1 %collective-permute-start = (f32[2,16,128]{2,1,0:T(8,128)S(1)}, f32[2,16,128]{2,1,0:T(8,128)S(1)}, u32[]{:S(2)}, u32[]{:S(2)}) collective-permute-start(f32[2,16,128]{2,1,0:T(8,128)S(1)} %get-tuple-element.26), channel_id=1, source_target_pairs={{0,4},{4,8},{8,12},{12,16},{16,20},{20,24},{24,28},{28,0},{1,5},{5... | collective-permute-start | bytes 49160 | tf_op jit(solution)/shard_map/ppermute | solution.py:374
  82.1 1.4 %collective-permute-start.1 = (f32[2,16,128]{2,1,0:T(8,128)S(1)}, f32[2,16,128]{2,1,0:T(8,128)S(1)}, u32[]{:S(2)}, u32[]{:S(2)}) collective-permute-start(f32[2,16,128]{2,1,0:T(8,128)S(1)} %get-tuple-element.26), channel_id=1, source_target_pairs={{0,28},{4,0},{8,4},{12,8},{16,12},{20,16},{24,20},{28,24},{1,29},{... | collective-permute-start | bytes 49160 | tf_op jit(solution)/shard_map/ppermute | solution.py:374
  83.5 5.8 %collective-permute-start.2 = (f32[72,128]{1,0:T(8,128)S(1)}, f32[72,128]{1,0:T(8,128)S(1)}, u32[]{:S(2)}, u32[]{:S(2)}) collective-permute-start(f32[72,128]{1,0:T(8,128)S(1)} %get-tuple-element.27), channel_id=1, source_target_pairs={{1,0},{2,1},{3,2},{5,4},{6,5},{7,6},{9,8},{10,9},{11,10},{13,12},{... | collective-permute-start | bytes 110600 | tf_op jit(solution)/shard_map/ppermute | solution.py:374
  89.4 4.9 %collective-permute-start.3 = (f32[72,128]{1,0:T(8,128)S(1)}, f32[72,128]{1,0:T(8,128)S(1)}, u32[]{:S(2)}, u32[]{:S(2)}) collective-permute-start(f32[72,128]{1,0:T(8,128)S(1)} %get-tuple-element.28), channel_id=1, source_target_pairs={{0,1},{1,2},{2,3},{4,5},{5,6},{6,7},{8,9},{9,10},{10,11},{12,13},{... | collective-permute-start | bytes 110600 | tf_op jit(solution)/shard_map/ppermute | solution.py:374
  94.2 1.1 copy-start.5
  97.8 0.9 copy-start.17
  98.7 0.6 copy-start.27
  99.3 28.2 %collective-permute-start.8 = (f32[72,128]{1,0:T(8,128)}, f32[72,128]{1,0:T(8,128)}, u32[]{:S(2)}, u32[]{:S(2)}) collective-permute-start(f32[72,128]{1,0:T(8,128)} %get-tuple-element.40), channel_id=1, source_target_pairs={{1,0},{2,1},{3,2},{5,4},{6,5},{7,6},{9,8},{10,9},{11,10},{13,12},{... | collective-permute-start | bytes 110600 | tf_op jit(solution)/shard_map/ppermute | solution.py:374
  100.6 26.9 %collective-permute-start.9 = (f32[72,128]{1,0:T(8,128)}, f32[72,128]{1,0:T(8,128)}, u32[]{:S(2)}, u32[]{:S(2)}) collective-permute-start(f32[72,128]{1,0:T(8,128)} %get-tuple-element.41), channel_id=1, source_target_pairs={{0,1},{1,2},{2,3},{4,5},{5,6},{6,7},{8,9},{9,10},{10,11},{12,13},{... | collective-permute-start | bytes 110600 | tf_op jit(solution)/shard_map/ppermute | solution.py:374
  106.1 20.7 %all-to-all-start.2 = ((f32[32,1,128]{2,1,0:T(1,128)}), f32[32,1,128]{2,1,0:T(1,128)S(1)}, u32[]{:S(2)}, u32[]{:S(2)}) async-start(f32[32,1,128]{2,1,0:T(1,128)} %bitcast.23), calls=%async_computation.2 | async-start | bytes 32768 | tf_op jit(solution)/shard_map/all_to_all | solution.py:476
  110.2 17.3 %collective-permute-start.6 = (f32[2,16,128]{2,1,0:T(8,128)}, f32[2,16,128]{2,1,0:T(8,128)}, u32[]{:S(2)}, u32[]{:S(2)}) collective-permute-start(f32[2,16,128]{2,1,0:T(8,128)} %copy-done.27), channel_id=1, source_target_pairs={{0,4},{4,8},{8,12},{12,16},{16,20},{20,24},{24,28},{28,0},{1,5},{5... | collective-permute-start | bytes 49160 | tf_op jit(solution)/shard_map/ppermute | solution.py:374
  110.5 17.0 %collective-permute-start.7 = (f32[2,16,128]{2,1,0:T(8,128)}, f32[2,16,128]{2,1,0:T(8,128)}, u32[]{:S(2)}, u32[]{:S(2)}) collective-permute-start(f32[2,16,128]{2,1,0:T(8,128)} %copy-done.27), channel_id=1, source_target_pairs={{0,28},{4,0},{8,4},{12,8},{16,12},{20,16},{24,20},{28,24},{1,29},{... | collective-permute-start | bytes 49160 | tf_op jit(solution)/shard_map/ppermute | solution.py:374
  112.9 1.1 copy-start.6
  114.0 2.3 %copy-start.9 = (f32[9216,128]{1,0:T(8,128)S(1)}, f32[9216,128]{1,0:T(8,128)}, u32[]{:S(2)}) copy-start(f32[9216,128]{1,0:T(8,128)} %copy-done.8) | copy-start | bytes 14155780
  124.6 2.2 %copy-start = (f32[9216,128]{1,0:T(8,128)}, f32[9216,128]{1,0:T(8,128)S(1)}, u32[]{:S(2)}) copy-start(f32[9216,128]{1,0:T(8,128)S(1)} %step.6.refs_12_) | copy-start | bytes 14155780
  127.5 2.3 %copy-start.1 = (f32[9216,128]{1,0:T(8,128)S(1)}, f32[9216,128]{1,0:T(8,128)}, u32[]{:S(2)}) copy-start(f32[9216,128]{1,0:T(8,128)} %copy-done) | copy-start | bytes 14155780
  129.8 1.1 copy-start.7
  130.9 1.1 copy-start.18
